TPU v7x, 32 devices: a whole 2x2x4 slice. The times are simulated.
32 devices in a mesh: req: 16 (over z, y, x), tp: 2 (over core).
Axes of the slice: x: 2, y: 2, z: 4, core: 2. Of those that a mesh axis runs over, the one named last changes fastest.
Arguments:
- vit_context: bfloat16 [8192, 4096], P('req', 'tp'), may hold values from -6 to 6
- vision_residual: bfloat16 [8192, 4096], P('req', 'tp'), may hold values from -75 to 75
- out_weight: bfloat16 [4096, 4096], P('tp', 'req'), may hold values from -0.09375 to 0.09375
- layer_scale: float32 [4096], P('tp'), may hold values from 0.2 to 2
- prompt: bfloat16 [16, 256, 4096], P('req', None, 'tp'), may hold values from -75 to 75
- prompt_len: int32 [16], P('req'), may hold values from 128 to 256
- image_at: int32 [16], P('req'), may hold values from 0 to 128
- grid_sizes: int32 [32, 2], replicated, may hold values from 7 to 8, as said below
- image_owner: int32 [32], replicated, may hold values from 0 to 15, as said below
- norm_gain: float32 [4096], replicated, may hold values from 0.5 to 1.5
- qkv_weight: bfloat16 [4096, 6144], P('req', 'tp'), may hold values from -0.09375 to 0.09375
Outputs:
- qkv: bfloat16 [6144, 6144], P('req', 'tp')
Inputs may be any that keep to these rules, and one draw needn't show every extreme that they name: `image_owner`: each request owns exactly 2 images. `grid_sizes`: each side is 7 or 8; in every draw the images of some request are all 8 by 8, so that request has exactly 128 merged rows.
All inputs are finite; a program needn't handle non-finite values.
Results may differ from a plain program's by a relative error of at most 0.008.
Values may be sent and summed in bfloat16 or wider, within the bound.
A program may use at most 64 MiB of HBM per device.

v0:
```python
import jax
import jax.numpy as jnp
from jax import lax
from jax.sharding import PartitionSpec as P

HEAD = 128
GROUP = 4
IMG_MAX = 128


def request_plan(grid_sizes, image_owner, requests):
    image_rows = grid_sizes[:, 0] * grid_sizes[:, 1]
    member = (image_owner[:, None] == jnp.arange(requests, dtype=jnp.int32)[None, :]).astype(
        jnp.int32
    )
    counts = jnp.sum(image_rows[:, None] * member, axis=0)
    starts = jnp.cumsum(counts) - counts
    return (counts, starts)


def rope_tables(count):
    half_size = HEAD // 2
    exponent = jnp.arange(half_size, dtype=jnp.float32) * (2.0 / HEAD)
    frequency = jnp.exp(-exponent * jnp.log(jnp.float32(500000.0)))
    angles = jnp.arange(count, dtype=jnp.float32)[:, None] * frequency[None, :]
    return (jnp.cos(angles), jnp.sin(angles))


def apply_rope(projected, cosine_table, sine_table):
    seq_rows = projected.shape[0]
    head_blocks = projected.reshape(seq_rows, -1, GROUP + 2, HEAD)
    turning = head_blocks[:, :, : GROUP + 1, :]
    first_half = turning[..., : HEAD // 2]
    second_half = turning[..., HEAD // 2 :]
    cosine_wide = cosine_table[:, None, None, :]
    sine_wide = sine_table[:, None, None, :]
    turned = jnp.concatenate(
        [
            first_half * cosine_wide - second_half * sine_wide,
            second_half * cosine_wide + first_half * sine_wide,
        ],
        axis=-1,
    )
    head_blocks = jnp.concatenate([turned, head_blocks[:, :, GROUP + 1 :, :]], axis=2)
    return head_blocks.reshape(seq_rows, -1)


def normalize(embedded, norm_gain):
    values = embedded.astype(jnp.float32)
    mean_square = jnp.mean(values * values, axis=-1, keepdims=True)
    return (values * lax.rsqrt(mean_square + 1e-05) * norm_gain[None, :]).astype(jnp.bfloat16)


def shards(
    vit_context,
    vision_residual,
    out_weight,
    layer_scale,
    prompt,
    prompt_len,
    image_at,
    grid_sizes,
    image_owner,
    norm_gain,
    qkv_weight,
):
    requests = lax.axis_size("req")
    device_index = lax.axis_index("req")
    feature_width = vit_context.shape[1]
    merged_context = jnp.mean(
        vit_context.astype(jnp.float32).reshape(-1, 4, feature_width), axis=1
    ).astype(jnp.bfloat16)
    merged_residual = jnp.mean(
        vision_residual.astype(jnp.float32).reshape(-1, 4, feature_width), axis=1
    )
    partial_value = jnp.dot(
        merged_context,
        lax.all_gather(out_weight, "req", axis=1, tiled=True),
        preferred_element_type=jnp.float32,
    )
    summed = lax.psum(partial_value.astype(jnp.bfloat16), "tp").astype(jnp.float32)
    own_share = lax.dynamic_slice_in_dim(
        summed, lax.axis_index("tp") * feature_width, feature_width, 1
    )
    merged = (merged_residual + layer_scale[None, :] * own_share).astype(jnp.bfloat16)
    merged_count = merged.shape[0]
    counts, starts = request_plan(grid_sizes, image_owner, requests)
    request_ends = starts + counts
    capacity = (IMG_MAX + requests - 1) // requests
    request_ids = jnp.arange(requests, dtype=jnp.int32)
    group_index = jnp.arange(merged_count, dtype=jnp.int32) * requests + device_index
    destination = jnp.sum((request_ends[None, :] <= group_index[:, None]).astype(jnp.int32), axis=1)
    owned_start = jnp.sum(
        jnp.where(destination[:, None] == request_ids[None, :], starts[None, :], 0), axis=1
    )
    target = destination * capacity + (group_index - owned_start) // requests
    usable = destination < requests
    send_slots = jnp.arange(requests * capacity, dtype=jnp.int32)
    placing = ((send_slots[:, None] == target[None, :]) & usable[None, :]).astype(jnp.bfloat16)
    outgoing = jnp.dot(placing, merged, preferred_element_type=jnp.float32).astype(jnp.bfloat16)
    arrived = lax.all_to_all(
        outgoing.reshape(requests, capacity, feature_width),
        "req",
        split_axis=0,
        concat_axis=0,
        tiled=True,
    )
    arrived = arrived.reshape(requests * capacity, feature_width)
    own_request = request_ids == device_index
    own_count = jnp.sum(jnp.where(own_request, counts, 0))
    own_start = jnp.sum(jnp.where(own_request, starts, 0))
    image_from = image_at[0]
    prompt_count = prompt_len[0]
    seq_slots = prompt.shape[1] + IMG_MAX
    slot_index = jnp.arange(seq_slots, dtype=jnp.int32)
    image_row = slot_index - image_from
    in_image = (image_row >= 0) & (image_row < own_count)
    is_live = slot_index < prompt_count + own_count
    from_prompt = is_live & jnp.logical_not(in_image)
    flat_index = (own_start + image_row) % requests * capacity + image_row // requests
    image_pick = ((flat_index[:, None] == send_slots[None, :]) & in_image[:, None]).astype(
        jnp.bfloat16
    )
    prompt_row = jnp.where(slot_index < image_from, slot_index, slot_index - own_count)
    prompt_ids = jnp.arange(prompt.shape[1], dtype=jnp.int32)
    prompt_pick = ((prompt_row[:, None] == prompt_ids[None, :]) & from_prompt[:, None]).astype(
        jnp.bfloat16
    )
    embedded = (
        jnp.dot(image_pick, arrived, preferred_element_type=jnp.float32)
        + jnp.dot(prompt_pick, prompt[0], preferred_element_type=jnp.float32)
    ).astype(jnp.bfloat16)
    gathered = lax.all_gather(embedded, "tp", axis=1, tiled=True)
    normed = normalize(gathered, norm_gain)
    projected = jnp.dot(
        normed,
        lax.all_gather(qkv_weight, "req", axis=0, tiled=True),
        preferred_element_type=jnp.float32,
    )
    cosine_table, sine_table = rope_tables(seq_slots)
    return apply_rope(projected, cosine_table, sine_table).astype(jnp.bfloat16)


def solution(mesh):
    in_specs = (
        P("req", "tp"),
        P("req", "tp"),
        P("tp", "req"),
        P("tp"),
        P("req", None, "tp"),
        P("req"),
        P("req"),
        P(),
        P(),
        P(),
        P("req", "tp"),
    )
    out_specs = P("req", "tp")
    return jax.shard_map(shards, mesh=mesh, in_specs=in_specs, out_specs=out_specs, check_vma=False)
```

profile of v0, /device:TPU:0, one launch (start us, length us, event | category | flops | bytes accessed | tf_op | source)
XLA Modules:
  0.0 616.2 jit_solution(16487979438478176217)
XLA Ops:
  6.5 0.7 all-gather.4.cloned.1.call-update
  7.3 4.8 reshape.201
  12.1 4.8 reduce_sum.78
  17.0 231.1 %all-gather.4.cloned.1.call-done = bf16[2048,4096]{1,0:T(8,128)(2,1)} async-done(((bf16[2048,256]{1,0:T(8,128)(2,1)}), bf16[2048,4096]{1,0:T(8,128)(2,1)}) %all-gather.4.cloned.1.call-update) | async-done | bytes 16777232 | tf_op jit(solution)/shard_map/all_gather | solution.py:78
  248.0 9.1 %convolution_convert_fusion = bf16[128,4096]{1,0:T(8,128)(2,1)} fusion(bf16[2048,4096]{1,0:T(8,128)(2,1)} %all-gather.4.cloned.1.call-done, f32[128,2048]{1,0:T(8,128)S(1)} %reduce_sum.78), kind=kOutput, calls=%fused_computation.5 | convolution fusion | flops 2148532224 | bytes 18874368 | tf_op jit(solution)/shard_map/dot_general | solution.py:76
  257.2 0.1 select_reduce_fusion.1
  257.3 0.1 copy.16
  257.4 0.1 reduce
  257.5 4.8 reshape.199
  262.3 5.0 reduce_sum.77
  267.3 0.1 convert_reduce_fusion
  267.4 0.7 fusion.39
  268.1 0.1 select_reduce_fusion
  268.2 6.9 %all-reduce.2.cloned.1.call-done = bf16[128,4096]{1,0:T(8,128)(2,1)} async-done(((bf16[128,4096]{1,0:T(8,128)(2,1)}), bf16[128,4096]{1,0:T(8,128)(2,1)}) %all-reduce.2.cloned.1.call-update) | async-done | bytes 1048592 | tf_op jit(solution)/shard_map/psum | solution.py:81
  275.1 2.2 fusion.7
  277.2 6.8 %all-to-all-start = ((bf16[16,8,2048]{2,1,0:T(8,128)(2,1)}), bf16[16,8,2048]{2,1,0:T(8,128)(2,1)S(1)}, u32[]{:S(2)}, u32[]{:S(2)}) async-start(bf16[16,8,2048]{2,1,0:T(8,128)(2,1)} %fusion.7), calls=%async_computation | async-start | bytes 1048576 | tf_op jit(solution)/shard_map/all_to_all | solution.py:101
  286.0 0.6 fusion.38
  286.5 0.6 subtract_select_fusion
  287.1 0.7 fusion.31
  287.8 11.7 %all-to-all-done = bf16[16,8,2048]{2,1,0:T(8,128)(2,1)S(1)} async-done(((bf16[16,8,2048]{2,1,0:T(8,128)(2,1)}), bf16[16,8,2048]{2,1,0:T(8,128)(2,1)S(1)}, u32[]{:S(2)}, u32[]{:S(2)}) %all-to-all-start) | async-done | bytes 524320 | tf_op jit(solution)/shard_map/all_to_all | solution.py:101
  299.5 0.6 fusion.10
  300.2 1.8 add_convert_fusion
  302.0 0.2 all-gather.8.cloned.1.call-start
  302.2 0.3 all-gather.8.cloned.1.call-update
  302.6 0.4 fusion.22
  303.0 9.6 %all-gather.6.cloned.1.call-done = bf16[384,4096]{1,0:T(8,128)(2,1)} async-done(((bf16[384,2048]{1,0:T(8,128)(2,1)}), bf16[384,4096]{1,0:T(8,128)(2,1)}) %all-gather.6.cloned.1.call-update) | async-done | bytes 3145744 | tf_op jit(solution)/shard_map/all_gather | solution.py:133
  312.7 2.6 fusion
  315.3 272.8 %all-gather.8.cloned.1.call-done = bf16[4096,3072]{1,0:T(8,128)(2,1)} async-done(((bf16[256,3072]{1,0:T(8,128)(2,1)}), bf16[4096,3072]{1,0:T(8,128)(2,1)}) %all-gather.8.cloned.1.call-update) | async-done | bytes 25165840 | tf_op jit(solution)/shard_map/all_gather | solution.py:137
  588.1 18.0 %fusion.3 = f32[384,3072]{0,1:T(8,128)S(1)} fusion(bf16[4096,3072]{1,0:T(8,128)(2,1)} %all-gather.8.cloned.1.call-done, bf16[384,4096]{1,0:T(8,128)(2,1)} %all-gather.6.cloned.1.call-done, f32[4096]{0:T(1024)S(1)} %copy-done.3, f32[384]{0:T(512)S(1)} %add_rsqrt_fusion), kind=kOutput, calls=%fused_computation.6 | convolution fusion | flops 9669967872 | bytes 33048064 | tf_op jit(solution)/shard_map/dot_general | solution.py:135
  606.2 0.6 subtract_convert_fusion
  606.8 0.3 pad_maximum_fusion
  607.1 2.6 copy.18
  (25 shorter events, 0.3 us)
Async XLA Ops:
  6.5 293.6 %copy-start = (bf16[1,256,2048]{2,1,0:T(8,128)(2,1)S(1)}, bf16[1,256,2048]{2,1,0:T(8,128)(2,1)}, u32[]{:S(2)}) copy-start(bf16[1,256,2048]{2,1,0:T(8,128)(2,1)} %param.15) | copy-start | bytes 3145732
  6.5 241.5 %all-gather.4.cloned.1.call-start = ((), (), s32[]{:S(2)}) async-start(), calls=%async_computation.1 | async-start | bytes 17825792 | tf_op jit(solution)/shard_map/all_gather | solution.py:78
  7.3 267.8 %all-reduce.2.cloned.1.call-start = ((), (), s32[]{:S(2)}) async-start(), calls=%async_computation.2 | async-start | bytes 2097152 | tf_op jit(solution)/shard_map/psum | solution.py:81
  12.1 4.9 copy-start.4
  16.9 240.2 %copy-start.5 = (s32[32]{0:T(128)S(1)}, s32[32]{0:T(128)}, u32[]{:S(2)}) copy-start(s32[32]{0:T(128)} %param.19) | copy-start | bytes 388
  262.3 12.8 %copy-start.2 = (f32[2048]{0:T(1024)S(1)}, f32[2048]{0:T(1024)}, u32[]{:S(2)}) copy-start(f32[2048]{0:T(1024)} %param.14) | copy-start | bytes 24580
  277.2 22.3 %all-to-all-start = ((bf16[16,8,2048]{2,1,0:T(8,128)(2,1)}), bf16[16,8,2048]{2,1,0:T(8,128)(2,1)S(1)}, u32[]{:S(2)}, u32[]{:S(2)}) async-start(bf16[16,8,2048]{2,1,0:T(8,128)(2,1)} %fusion.7), calls=%async_computation | async-start | bytes 1048576 | tf_op jit(solution)/shard_map/all_to_all | solution.py:101
  284.1 28.6 %all-gather.6.cloned.1.call-start = ((), (), s32[]{:S(2)}) async-start(), calls=%async_computation.3 | async-start | bytes 4718592 | tf_op jit(solution)/shard_map/all_gather | solution.py:133
  302.0 286.1 %copy-start.3 = (f32[4096]{0:T(1024)S(1)}, f32[4096]{0:T(1024)}, u32[]{:S(2)}) copy-start(f32[4096]{0:T(1024)} %param.20) | copy-start | bytes 49156
  302.0 286.1 %all-gather.8.cloned.1.call-start = ((), (), s32[]{:S(2)}) async-start(), calls=%async_computation.4 | async-start | bytes 26738688 | tf_op jit(solution)/shard_map/all_gather | solution.py:137
  606.8 2.9 copy-start.1
Sparse Core Ops, SparseCore 0:
  10.1 237.9 all-gather.3
  257.3 17.7 all-reduce.1
  302.1 10.5 all-gather.5
  315.7 272.3 all-gather.7
where the time goes:
time: 617 us; the launch traced here: 616 us
  waiting for transfers between devices  533 us (86%)
  matrix products  31.7 us (5%)
  other arithmetic  16.8 us (3%)
  between operations  15.1 us (2%)
  local copies, waits for them, and re-layouts  12.3 us (2%)
  starting transfers between devices  7.1 us (1%)
    all_gather x1, waiting for transfers between devices, shards(): lax.all_gather(qkv_weight, 'req', axis=0, tiled=True)  273 us
    all_gather x1, waiting for transfers between devices, shards(): lax.all_gather(out_weight, 'req', axis=1, tiled=True)  231 us
    dot_general x1, matrix products, shards(): jnp.dot(normed, lax.all_gather(qkv_weight, 'req', axis=0, tiled=True), pr...  18 us
  transfers between devices with their start and end apart: 5, of which 5 were waited for; matrix products, arithmetic and copies ran while one was open for 4% of the time, Pallas kernels for 0%

commit v1 on v0

--- a/solution.py
+++ b/solution.py
@@ -45,12 +45,6 @@
     return head_blocks.reshape(seq_rows, -1)
 
 
-def normalize(embedded, norm_gain):
-    values = embedded.astype(jnp.float32)
-    mean_square = jnp.mean(values * values, axis=-1, keepdims=True)
-    return (values * lax.rsqrt(mean_square + 1e-05) * norm_gain[None, :]).astype(jnp.bfloat16)
-
-
 def shards(
     vit_context,
     vision_residual,
@@ -66,7 +60,24 @@
 ):
     requests = lax.axis_size("req")
     device_index = lax.axis_index("req")
+    tp_index = lax.axis_index("tp")
     feature_width = vit_context.shape[1]
+    plane = qkv_weight.shape[1] // ((GROUP + 2) * HEAD)
+    depth = requests // plane
+    in_plane = [[d * plane + i for i in range(plane)] for d in range(depth)]
+    in_depth = [[d * plane + i for d in range(depth)] for i in range(plane)]
+    weight_rows = qkv_weight.shape[0]
+    weight_parts = jnp.swapaxes(qkv_weight.reshape(weight_rows, plane, -1), 0, 1)
+    weight_parts = lax.all_to_all(
+        weight_parts, "req", split_axis=0, concat_axis=0, axis_index_groups=in_plane, tiled=True
+    )
+    decoder_weight = lax.all_gather(
+        weight_parts.reshape(plane * weight_rows, -1),
+        "req",
+        axis=0,
+        axis_index_groups=in_depth,
+        tiled=True,
+    )
     merged_context = jnp.mean(
         vit_context.astype(jnp.float32).reshape(-1, 4, feature_width), axis=1
     ).astype(jnp.bfloat16)
@@ -74,14 +85,21 @@
         vision_residual.astype(jnp.float32).reshape(-1, 4, feature_width), axis=1
     )
     partial_value = jnp.dot(
-        merged_context,
-        lax.all_gather(out_weight, "req", axis=1, tiled=True),
+        lax.all_gather(merged_context, "req", axis=0, axis_index_groups=in_depth, tiled=True),
+        lax.all_gather(out_weight, "req", axis=1, axis_index_groups=in_plane, tiled=True),
         preferred_element_type=jnp.float32,
     )
-    summed = lax.psum(partial_value.astype(jnp.bfloat16), "tp").astype(jnp.float32)
-    own_share = lax.dynamic_slice_in_dim(
-        summed, lax.axis_index("tp") * feature_width, feature_width, 1
+    returned = lax.all_to_all(
+        partial_value.astype(jnp.bfloat16).reshape(depth, merged_context.shape[0], -1),
+        "req",
+        split_axis=0,
+        concat_axis=0,
+        axis_index_groups=in_depth,
+        tiled=True,
     )
+    returned = jnp.swapaxes(returned, 0, 1).reshape(merged_context.shape[0], -1)
+    summed = lax.psum(returned, "tp").astype(jnp.float32)
+    own_share = lax.dynamic_slice_in_dim(summed, tp_index * feature_width, feature_width, 1)
     merged = (merged_residual + layer_scale[None, :] * own_share).astype(jnp.bfloat16)
     merged_count = merged.shape[0]
     counts, starts = request_plan(grid_sizes, image_owner, requests)
@@ -130,15 +148,27 @@
         jnp.dot(image_pick, arrived, preferred_element_type=jnp.float32)
         + jnp.dot(prompt_pick, prompt[0], preferred_element_type=jnp.float32)
     ).astype(jnp.bfloat16)
-    gathered = lax.all_gather(embedded, "tp", axis=1, tiled=True)
-    normed = normalize(gathered, norm_gain)
-    projected = jnp.dot(
-        normed,
-        lax.all_gather(qkv_weight, "req", axis=0, tiled=True),
-        preferred_element_type=jnp.float32,
+    values = embedded.astype(jnp.float32)
+    square_sum = lax.psum(jnp.sum(values * values, axis=-1, keepdims=True), "tp")
+    mean_square = square_sum / (feature_width * lax.axis_size("tp"))
+    own_gain = lax.dynamic_slice_in_dim(norm_gain, tp_index * feature_width, feature_width, 0)
+    normed = (values * lax.rsqrt(mean_square + 1e-05) * own_gain[None, :]).astype(jnp.bfloat16)
+    normed = lax.all_gather(normed, "req", axis=0, axis_index_groups=in_plane, tiled=True)
+    normed = lax.all_gather(normed, "tp", axis=1, tiled=True)
+    projected = jnp.dot(normed, decoder_weight, preferred_element_type=jnp.float32)
+    cosine_table, sine_table = rope_tables(seq_slots)
+    cosine_table = jnp.tile(cosine_table, (plane, 1))
+    sine_table = jnp.tile(sine_table, (plane, 1))
+    turned = apply_rope(projected, cosine_table, sine_table).astype(jnp.bfloat16)
+    turned = lax.all_to_all(
+        turned.reshape(plane, seq_slots, -1),
+        "req",
+        split_axis=0,
+        concat_axis=0,
+        axis_index_groups=in_plane,
+        tiled=True,
     )
-    cosine_table, sine_table = rope_tables(seq_slots)
-    return apply_rope(projected, cosine_table, sine_table).astype(jnp.bfloat16)
+    return jnp.swapaxes(turned, 0, 1).reshape(seq_slots, -1)
 
 
 def solution(mesh):

time: 617 us -> 498 us (0.81)
  waiting for transfers between devices: 533 us -> 325 us
  blocking collectives: 0 us -> 75.2 us
  local copies, waits for them, and re-layouts: 12.3 us -> 28.9 us
  matrix products: 31.7 us -> 23.5 us
    all_gather x3 -> x5, waiting for transfers between devices: 514 us -> 280 us  [the longest x1 116 us: shards(): lax.all_gather(weight_parts.reshape(plane * weight_rows, -1), 'req', axis...]
    all_to_all x0 -> x2, blocking collectives: none -> 72.7 us  [the longest x1 40.3 us: shards(): lax.all_to_all(weight_parts, 'req', split_axis=0, concat_axis=0, axis_ind...]
    all_to_all x0 -> x1, waiting for transfers between devices: none -> 25.7 us  [shards(): lax.all_to_all(partial_value.astype(jnp.bfloat16).reshape(depth, merged_c...]
    dot_general x2, matrix products: 27.1 us -> 20 us  [the longest x1 14.8 us: shards(): jnp.dot(normed, decoder_weight, preferred_element_type=jnp.float32)]
  transfers between devices with their start and end apart: 5 -> 8, of which waited for: 5 -> 8; matrix products, arithmetic and copies ran while one was open for 4% -> 3% of each run, Pallas kernels for 0% -> 0%
where the time goes in v1:
time: 498 us; the launch traced here: 497 us
  waiting for transfers between devices  325 us (65%)
  blocking collectives  75.2 us (15%)
  local copies, waits for them, and re-layouts  28.9 us (6%)
  matrix products  23.5 us (5%)
  other arithmetic  16.6 us (3%)
  between operations  15.6 us (3%)
  starting transfers between devices  11.7 us (2%)
    all_gather x1, waiting for transfers between devices, shards(): lax.all_gather(weight_parts.reshape(plane * weight_rows, -1), 'req', axis...  116 us
    all_gather x1, waiting for transfers between devices, shards(): lax.all_gather(out_weight, 'req', axis=1, axis_index_groups=in_plane, til...  53.1 us
    all_gather x1, waiting for transfers between devices, shards(): lax.all_gather(merged_context, 'req', axis=0, axis_index_groups=in_depth,...  48 us
    all_to_all x1, blocking collectives, shards(): lax.all_to_all(weight_parts, 'req', split_axis=0, concat_axis=0, axis_ind...  40.3 us
    all_gather x1, waiting for transfers between devices, shards(): lax.all_gather(normed, 'req', axis=0, axis_index_groups=in_plane, tiled=T...  38.3 us
    all_to_all x1, blocking collectives, shards(): lax.all_to_all(turned.reshape(plane, seq_slots, -1), 'req', split_axis=0,...  32.5 us
    all_to_all x1, waiting for transfers between devices, shards(): lax.all_to_all(partial_value.astype(jnp.bfloat16).reshape(depth, merged_c...  25.7 us
    all_gather x1, waiting for transfers between devices, shards(): normed = lax.all_gather(normed, 'tp', axis=1, tiled=True)  24.7 us
  transfers between devices with their start and end apart: 8, of which 8 were waited for; matrix products, arithmetic and copies ran while one was open for 3% of the time, Pallas kernels for 0%

profile of v1, /device:TPU:0, one launch (start us, length us, event | category | flops | bytes accessed | tf_op | source)
XLA Modules:
  0.0 496.9 jit_solution(6401885168935334047)
XLA Ops:
  6.5 4.8 reshape.235
  11.4 4.8 reduce_sum.78
  16.2 0.9 multiply_convert_fusion
  17.9 48.0 %all-gather.6.cloned.1.call-done = bf16[512,2048]{1,0:T(8,128)(2,1)} async-done(((bf16[128,2048]{1,0:T(8,128)(2,1)}), bf16[512,2048]{1,0:T(8,128)(2,1)}) %all-gather.6.cloned.1.call-update) | async-done | bytes 2097168 | tf_op jit(solution)/shard_map/all_gather | solution.py:88
  65.9 53.1 %all-gather.8.cloned.1.call-done = bf16[2048,1024]{1,0:T(8,128)(2,1)} async-done(((bf16[2048,256]{1,0:T(8,128)(2,1)}), bf16[2048,1024]{1,0:T(8,128)(2,1)}) %all-gather.8.cloned.1.call-update) | async-done | bytes 4194320 | tf_op jit(solution)/shard_map/all_gather | solution.py:89
  119.0 5.1 %convolution_convert_fusion.1 = bf16[512,1024]{1,0:T(8,128)(2,1)S(1)} fusion(bf16[512,2048]{1,0:T(8,128)(2,1)} %all-gather.6.cloned.1.call-done, bf16[2048,1024]{1,0:T(8,128)(2,1)} %all-gather.8.cloned.1.call-done), kind=kOutput, calls=%fused_computation.11 | convolution fusion | flops 2148007936 | bytes 7340032 | tf_op jit(solution)/shard_map/dot_general | solution.py:87
  124.2 1.3 copy.37
  125.5 4.7 all-to-all-start
  130.3 25.7 %all-to-all-done = bf16[4,128,1024]{1,2,0:T(8,128)(2,1)S(1)} async-done(((bf16[4,128,1024]{1,2,0:T(8,128)(2,1)}), bf16[4,128,1024]{1,2,0:T(8,128)(2,1)S(1)}, u32[]{:S(2)}, u32[]{:S(2)}) %all-to-all-start) | async-done | bytes 1048608 | tf_op jit(solution)/shard_map/all_to_all | solution.py:92
  156.0 1.3 copy.38
  157.7 4.8 reshape.233
  162.4 5.0 %reduce_sum.77 = f32[128,2048]{1,0:T(8,128)S(1)} reduce(f32[128,4,2048]{2,1,0:T(4,128)} %reshape.233, f32[]{:T(128)} %constant.66.clone.1), dimensions={1}, to_apply=%region_6.7 | reduce | flops 786432 | bytes 5242884 | tf_op jit(solution)/shard_map/reduce_sum | solution.py:84
  168.3 6.9 %all-reduce.2.cloned.1.call-done = bf16[128,4096]{1,0:T(8,128)(2,1)} async-done(((bf16[128,4096]{1,0:T(8,128)(2,1)}), bf16[128,4096]{1,0:T(8,128)(2,1)}) %all-reduce.2.cloned.1.call-update) | async-done | bytes 1048592 | tf_op jit(solution)/shard_map/psum | solution.py:101
  175.2 2.2 fusion.3
  177.4 6.8 %all-to-all-start.1 = ((bf16[16,8,2048]{2,1,0:T(8,128)(2,1)}), bf16[16,8,2048]{2,1,0:T(8,128)(2,1)S(1)}, u32[]{:S(2)}, u32[]{:S(2)}) async-start(bf16[16,8,2048]{2,1,0:T(8,128)(2,1)} %fusion.3), calls=%async_computation.1 | async-start | bytes 1048576 | tf_op jit(solution)/shard_map/all_to_all | solution.py:119
  188.0 11.6 %all-to-all-done.1 = bf16[16,8,2048]{2,1,0:T(8,128)(2,1)S(1)} async-done(((bf16[16,8,2048]{2,1,0:T(8,128)(2,1)}), bf16[16,8,2048]{2,1,0:T(8,128)(2,1)S(1)}, u32[]{:S(2)}, u32[]{:S(2)}) %all-to-all-start.1) | async-done | bytes 524320 | tf_op jit(solution)/shard_map/all_to_all | solution.py:119
  200.3 0.8 fusion
  201.1 2.5 psum.15
  203.6 1.6 fusion.2
  205.3 1.3 copy-done.2
  206.6 1.6 copy.39
  208.2 40.3 %all_to_all.20 = bf16[4,256,768]{1,2,0:T(8,128)(2,1)S(1)} all-to-all(bf16[4,256,768]{1,2,0:T(8,128)(2,1)} %bitcast.49), channel_id=1, replica_groups={{0,2,4,6},{8,10,12,14},{16,18,20,22},{24,26,28,30},{1,3,5,7},{9,11,13,1..., dimensions={0} | all-to-all | bytes 3145728 | tf_op jit(solution)/shard_map/all_to_all | solution.py:71
  248.4 1.6 copy.40
  250.1 38.3 %all-gather.10.cloned.1.call-done = bf16[1536,2048]{1,0:T(8,128)(2,1)} async-done(((bf16[384,2048]{1,0:T(8,128)(2,1)}), bf16[1536,2048]{1,0:T(8,128)(2,1)}) %all-gather.10.cloned.1.call-update) | async-done | bytes 6291472 | tf_op jit(solution)/shard_map/all_gather | solution.py:156
  289.1 116.2 %all-gather.14.cloned.1.call-done = bf16[4096,768]{1,0:T(8,128)(2,1)} async-done(((bf16[1024,768]{1,0:T(8,128)(2,1)}), bf16[4096,768]{1,0:T(8,128)(2,1)}) %all-gather.14.cloned.1.call-update) | async-done | bytes 6291472 | tf_op jit(solution)/shard_map/all_gather | solution.py:74
  405.3 24.7 %all-gather.12.cloned.1.call-done = bf16[1536,4096]{1,0:T(8,128)(2,1)} async-done(((bf16[1536,2048]{1,0:T(8,128)(2,1)}), bf16[1536,4096]{1,0:T(8,128)(2,1)}) %all-gather.12.cloned.1.call-update) | async-done | bytes 12582928 | tf_op jit(solution)/shard_map/all_gather | solution.py:157
  430.0 14.8 %fusion.40 = f32[1536,768]{0,1:T(8,128)S(1)} fusion(bf16[1536,4096]{1,0:T(8,128)(2,1)} %all-gather.12.cloned.1.call-done, bf16[4096,768]{1,0:T(8,128)(2,1)} %all-gather.14.cloned.1.call-done), kind=kOutput, calls=%fused_computation.79 | convolution fusion | flops 9663676416 | bytes 23592960 | tf_op jit(solution)/shard_map/dot_general | solution.py:158
  445.7 2.1 convert_element_type.47
  447.8 4.1 copy.41
  451.9 32.5 %all_to_all.21 = bf16[4,384,768]{2,1,0:T(8,128)(2,1)} all-to-all(bf16[4,384,768]{2,1,0:T(8,128)(2,1)S(1)} %copy.41), channel_id=1, replica_groups={{0,2,4,6},{8,10,12,14},{16,18,20,22},{24,26,28,30},{1,3,5,7},{9,11,13,1..., dimensions={0} | all-to-all | bytes 4718592 | tf_op jit(solution)/shard_map/all_to_all | solution.py:163
  484.4 3.0 copy.42
  487.4 2.6 copy.43
  (51 shorter events, 6.2 us)
Async XLA Ops:
  6.5 193.8 %copy-start = (bf16[1,256,2048]{2,1,0:T(8,128)(2,1)S(1)}, bf16[1,256,2048]{2,1,0:T(8,128)(2,1)}, u32[]{:S(2)}) copy-start(bf16[1,256,2048]{2,1,0:T(8,128)(2,1)} %param.15) | copy-start | bytes 3145732
  6.5 59.4 %all-gather.6.cloned.1.call-start = ((), (), s32[]{:S(2)}) async-start(), calls=%async_computation.4 | async-start | bytes 2621440 | tf_op jit(solution)/shard_map/all_gather | solution.py:88
  17.1 101.9 %all-gather.8.cloned.1.call-start = ((), (), s32[]{:S(2)}) async-start(), calls=%async_computation.5 | async-start | bytes 5242880 | tf_op jit(solution)/shard_map/all_gather | solution.py:89
  124.2 6.1 %copy-start.4 = (s32[32,2]{0,1:T(2,128)S(1)}, s32[32,2]{0,1:T(2,128)}, u32[]{:S(2)}) copy-start(s32[32,2]{0,1:T(2,128)} %param.18) | copy-start | bytes 772
  125.5 31.8 %copy-start.5 = (s32[32]{0:T(128)S(1)}, s32[32]{0:T(128)}, u32[]{:S(2)}) copy-start(s32[32]{0:T(128)} %param.19) | copy-start | bytes 388
  125.5 30.5 %all-to-all-start = ((bf16[4,128,1024]{1,2,0:T(8,128)(2,1)}), bf16[4,128,1024]{1,2,0:T(8,128)(2,1)S(1)}, u32[]{:S(2)}, u32[]{:S(2)}) async-start(bf16[4,128,1024]{1,2,0:T(8,128)(2,1)} %copy.37), calls=%async_computation | async-start | bytes 2097152 | tf_op jit(solution)/shard_map/all_to_all | solution.py:92
  130.3 45.0 %all-reduce.2.cloned.1.call-start = ((), (), s32[]{:S(2)}) async-start(), calls=%async_computation.6 | async-start | bytes 2097152 | tf_op jit(solution)/shard_map/psum | solution.py:101
  162.4 12.8 %copy-start.3 = (f32[2048]{0:T(1024)S(1)}, f32[2048]{0:T(1024)}, u32[]{:S(2)}) copy-start(f32[2048]{0:T(1024)} %param.14) | copy-start | bytes 24580
  177.4 22.3 %all-to-all-start.1 = ((bf16[16,8,2048]{2,1,0:T(8,128)(2,1)}), bf16[16,8,2048]{2,1,0:T(8,128)(2,1)S(1)}, u32[]{:S(2)}, u32[]{:S(2)}) async-start(bf16[16,8,2048]{2,1,0:T(8,128)(2,1)} %fusion.3), calls=%async_computation.1 | async-start | bytes 1048576 | tf_op jit(solution)/shard_map/all_to_all | solution.py:119
  184.2 104.2 %all-gather.10.cloned.1.call-start = ((), (), s32[]{:S(2)}) async-start(), calls=%async_computation.7 | async-start | bytes 7864320 | tf_op jit(solution)/shard_map/all_gather | solution.py:156
  200.3 3.3 dynamic-slice-start
  205.2 1.4 copy-start.2
  205.2 200.1 %all-gather.14.cloned.1.call-start = ((), (), s32[]{:S(2)}) async-start(), calls=%async_computation.9 | async-start | bytes 7864320 | tf_op jit(solution)/shard_map/all_gather | solution.py:74
  250.1 179.9 %all-gather.12.cloned.1.call-start = ((), (), s32[]{:S(2)}) async-start(), calls=%async_computation.8 | async-start | bytes 18874368 | tf_op jit(solution)/shard_map/all_gather | solution.py:157
  487.4 2.6 copy-start.1
Sparse Core Ops, SparseCore 0:
  17.2 48.6 all-gather.5
  67.7 51.2 all-gather.7
  157.4 17.7 all-reduce.1
  205.3 83.0 all-gather.9
  289.9 115.3 all-gather.13
  406.8 23.1 all-gather.11

commit v2 on v1

--- a/solution.py
+++ b/solution.py
@@ -1,6 +1,10 @@
+import functools
+
 import jax
 import jax.numpy as jnp
 from jax import lax
+from jax.experimental import pallas as pl
+from jax.experimental.pallas import tpu as pltpu
 from jax.sharding import PartitionSpec as P
 
 HEAD = 128
@@ -45,7 +49,7 @@
     return head_blocks.reshape(seq_rows, -1)
 
 
-def shards(
+def collective_shards(
     vit_context,
     vision_residual,
     out_weight,
@@ -171,7 +175,573 @@
     return jnp.swapaxes(turned, 0, 1).reshape(seq_slots, -1)
 
 
+MESH = pl.DeviceIdType.MESH
+BF16 = jnp.bfloat16
+F32 = jnp.float32
+
+
+def dot(a, b):
+    return jnp.dot(a, b, preferred_element_type=F32)
+
+
+def fused_kernel(
+    dims,
+    context,
+    residual,
+    out_weight,
+    scale,
+    prompt,
+    gain,
+    qkv_weight,
+    averaging,
+    place_left,
+    place_right,
+    pick_left,
+    pick_right,
+    prompt_pick,
+    cosine,
+    sine,
+    out,
+    slab,
+    out_slab,
+    blocks,
+    partials,
+    returned,
+    mean_residual,
+    merged,
+    outgoing,
+    arrived,
+    embedded,
+    squares,
+    normed,
+    total,
+    turned,
+    slab_in_send,
+    slab_in_recv,
+    slab_local,
+    slab_send,
+    slab_recv,
+    out_slab_send,
+    out_slab_recv,
+    out_slab_local,
+    block_send,
+    block_recv,
+    partial_send,
+    partial_recv,
+    place_send,
+    place_recv,
+    square_send,
+    square_recv,
+    normed_send,
+    normed_recv,
+    cross_send,
+    turned_send,
+    turned_recv,
+    turned_local,
+):
+    requests, cores, plane, depth = dims
+    req = lax.axis_index("req")
+    core = lax.axis_index("tp")
+    level = req // plane
+    spot = req % plane
+    sibling = 1 - core
+    rows = blocks.shape[1]
+    width = blocks.shape[2]
+    depth_rows = qkv_weight.shape[0]
+    share = slab.shape[-1]
+    columns = out_weight.shape[1]
+    seq = out.shape[0]
+    half = width // 2
+    held = depth // cores
+    others = [
+        ((spot // 2 + ry) % 2) * 2 + (spot % 2 + rx) % 2 for ry, rx in ((0, 1), (1, 0), (1, 1))
+    ]
+
+    def remote(src, dst, send, recv, to_req, to_core):
+        return pltpu.make_async_remote_copy(
+            src_ref=src,
+            dst_ref=dst,
+            send_sem=send,
+            recv_sem=recv,
+            device_id=(to_req, to_core),
+            device_id_type=MESH,
+        )
+
+    def arrive(dst, recv):
+        remote(dst, dst, slab_local, recv, req, sibling).wait_recv()
+
+    barrier = pltpu.get_barrier_semaphore()
+    count = requests * cores
+
+    @pl.loop(1, count)
+    def _(offset):
+        at = (req * cores + core + offset) % count
+        pl.semaphore_signal(
+            barrier, inc=1, device_id=(at // cores, at % cores), device_id_type=MESH
+        )
+
+    pl.semaphore_wait(barrier, count - 1)
+
+    out_sends = []
+    for i, other in enumerate(others):
+        out_sends.append(
+            remote(
+                out_weight,
+                out_slab.at[spot],
+                out_slab_send.at[i],
+                out_slab_recv.at[spot],
+                level * plane + other,
+                core,
+            )
+        )
+        out_sends[-1].start()
+    out_own = pltpu.make_async_copy(out_weight, out_slab.at[spot], out_slab_local)
+    out_own.start()
+
+    for i in range(width // 512):
+        cols = slice(i * 512, (i + 1) * 512)
+        blocks[level, :, cols] = dot(averaging[...], context[:, cols]).astype(BF16)
+
+    def pass_on(buffer, send, recv, hop, first):
+        if hop > 1:
+
+            @pl.when(level - (hop - 1) >= 0)
+            def _():
+                arrive(buffer.at[level - (hop - 1)], recv.at[level - (hop - 1)])
+
+            @pl.when(level + (hop - 1) < depth)
+            def _():
+                arrive(buffer.at[level + (hop - 1)], recv.at[level + (hop - 1)])
+
+        if hop == depth:
+            return
+
+        @pl.when((level - (hop - 1) >= 0) & (level + 1 < depth))
+        def _():
+            at = level - (hop - 1)
+            remote(
+                buffer.at[at], buffer.at[at], send.at[hop - 1, 0], recv.at[at], req + plane, core
+            ).start()
+
+        @pl.when((level + (hop - 1) < depth) & (level - 1 >= 0))
+        def _():
+            at = level + (hop - 1)
+            remote(
+                buffer.at[at], buffer.at[at], send.at[hop - 1, 1], recv.at[at], req - plane, core
+            ).start()
+
+    def passed(buffer, send, recv):
+        for hop in range(1, depth):
+
+            @pl.when((level - (hop - 1) >= 0) & (level + 1 < depth))
+            def _():
+                at = level - (hop - 1)
+                remote(
+                    buffer.at[at], buffer.at[at], send.at[hop - 1, 0], recv.at[at], req, sibling
+                ).wait_send()
+
+            @pl.when((level + (hop - 1) < depth) & (level - 1 >= 0))
+            def _():
+                at = level + (hop - 1)
+                remote(
+                    buffer.at[at], buffer.at[at], send.at[hop - 1, 1], recv.at[at], req, sibling
+                ).wait_send()
+
+    pass_on(blocks, block_send, block_recv, 1, True)
+
+    slab_sends = []
+    for i, other in enumerate(others):
+        at = pl.multiple_of(other * share, share)
+        slab_sends.append(
+            remote(
+                qkv_weight.at[:, pl.ds(at, share)],
+                slab.at[level, spot],
+                slab_in_send.at[i],
+                slab_in_recv.at[spot],
+                level * plane + other,
+                core,
+            )
+        )
+        slab_sends[-1].start()
+    slab_own = pltpu.make_async_copy(
+        qkv_weight.at[:, pl.ds(pl.multiple_of(spot * share, share), share)],
+        slab.at[level, spot],
+        slab_local,
+    )
+    slab_own.start()
+
+    for i in range(width // 512):
+        cols = slice(i * 512, (i + 1) * 512)
+        mean_residual[:, cols] = dot(averaging[...], residual[:, cols])
+
+    for hop in range(2, depth + 1):
+        pass_on(blocks, block_send, block_recv, hop, True)
+    passed(blocks, block_send, block_recv)
+
+    slab_own.wait()
+    for other in others:
+        arrive(slab.at[level, other], slab_in_recv.at[other])
+    pass_on(slab, slab_send, slab_recv, 1, False)
+
+    out_own.wait()
+    for other in others:
+        arrive(out_slab.at[other], out_slab_recv.at[other])
+
+    owner_core = level // held
+    lane = level % held
+
+    @pl.loop(0, depth)
+    def _(step):
+        target = (level + 1 + step) % depth
+        for i in range(plane):
+            partials[target, :, i * columns : (i + 1) * columns] = dot(
+                blocks[target], out_slab[i]
+            ).astype(BF16)
+        own = (target == level) & (owner_core == core)
+
+        @pl.when(own)
+        def _():
+            pltpu.make_async_copy(
+                partials.at[target], returned.at[lane, core], partial_recv.at[lane, core]
+            ).start()
+
+        @pl.when(jnp.logical_not(own))
+        def _():
+            remote(
+                partials.at[target],
+                returned.at[lane, core],
+                partial_send.at[target],
+                partial_recv.at[lane, core],
+                target * plane + spot,
+                owner_core,
+            ).start()
+
+    for i in range(held):
+        for j in range(cores):
+            arrive(returned.at[i, j], partial_recv.at[i, j])
+    for i in range(held):
+        cols = slice(i * half, (i + 1) * half)
+        added = returned[i, 0].astype(F32)
+        for j in range(1, cores):
+            added = added + returned[i, j].astype(F32)
+        merged[:, cols] = (mean_residual[:, cols] + scale[:, cols] * added).astype(BF16)
+
+    placed = dot(place_left[...], merged[:, :half]) + dot(place_right[...], merged[:, half:])
+    outgoing[...] = placed.astype(BF16).reshape(outgoing.shape)
+
+    @pl.loop(1, requests)
+    def _(offset):
+        to = (req + offset) % requests
+        remote(
+            outgoing.at[to], arrived.at[req], place_send.at[to], place_recv.at[req], to, core
+        ).start()
+
+    place_own = pltpu.make_async_copy(outgoing.at[req], arrived.at[req], place_send.at[req])
+    place_own.start()
+    for i in range(2):
+        cols = slice(i * half, (i + 1) * half)
+        embedded[:, cols] = dot(prompt_pick[...], prompt[:, cols])
+    place_own.wait()
+
+    @pl.loop(1, requests)
+    def _(offset):
+        source = (req + offset) % requests
+        arrive(arrived.at[source], place_recv.at[source])
+
+    square_sum = jnp.zeros((seq, 1), F32)
+    for i, pick in enumerate((pick_left, pick_right)):
+        cols = slice(i * half, (i + 1) * half)
+        images = arrived[...].reshape(arrived.shape[0] * arrived.shape[1], half)
+        values = embedded[:, cols] + dot(pick[...], images)
+        embedded[:, cols] = values
+        square_sum = square_sum + jnp.sum(values * values, axis=-1, keepdims=True)
+    squares[0] = jnp.broadcast_to(square_sum, squares.shape[1:])
+    square_copy = remote(squares.at[0], squares.at[1], square_send, square_recv, req, sibling)
+    square_copy.start()
+    square_copy.wait()
+    mean_square = (squares[0, :, :1] + squares[1, :, :1]) / (width * cores)
+    factor = lax.rsqrt(mean_square + 1e-05)
+    for i in range(2):
+        cols = slice(i * half, (i + 1) * half)
+        normed[spot, core, :, cols] = (embedded[:, cols] * factor * gain[:, cols]).astype(BF16)
+
+    normed_sends = []
+    for i, other in enumerate(others):
+        normed_sends.append(
+            remote(
+                normed.at[spot, core],
+                normed.at[spot, core],
+                normed_send.at[i],
+                normed_recv.at[spot, core],
+                level * plane + other,
+                core,
+            )
+        )
+        normed_sends[-1].start()
+
+    def cross(place, i):
+        copy = remote(
+            normed.at[place, core],
+            normed.at[place, core],
+            cross_send.at[i],
+            normed_recv.at[place, core],
+            req,
+            sibling,
+        )
+        copy.start()
+        normed_sends.append(copy)
+
+    cross(spot, 0)
+    pass_on(slab, slab_send, slab_recv, 2, False)
+    for hop in range(3, depth):
+        pass_on(slab, slab_send, slab_recv, hop, False)
+    for i, other in enumerate(others):
+        arrive(normed.at[other, core], normed_recv.at[other, core])
+        cross(other, i + 1)
+    for place in [spot] + others:
+        arrive(normed.at[place, sibling], normed_recv.at[place, sibling])
+
+    tile = 256
+    level_rows = plane * depth_rows
+
+    def multiply(at, first):
+        part = at // held
+        base = pl.multiple_of((at % held) * level_rows, level_rows)
+
+        @pl.loop(0, plane)
+        def _(place):
+            a = normed[place, part, :, pl.ds(base, level_rows)]
+            for n in range(share // tile):
+                cols = slice(n * tile, (n + 1) * tile)
+                b = slab[at, :, :, cols].reshape(level_rows, tile)
+                if first:
+                    total[place, :, cols] = dot(a, b)
+                else:
+                    total[place, :, cols] += dot(a, b)
+
+    multiply(level, True)
+    for hop in range(1, depth):
+        if hop == depth - 1:
+            pass_on(slab, slab_send, slab_recv, depth, False)
+
+        @pl.when(level - hop >= 0)
+        def _():
+            multiply(level - hop, False)
+
+        @pl.when(level + hop < depth)
+        def _():
+            multiply(level + hop, False)
+
+    turned_sends = []
+    here = pl.ds(pl.multiple_of(spot * share, share), share)
+    for i, place in enumerate(others + [spot]):
+        for head in range(share // HEAD):
+            cols = slice(head * HEAD, (head + 1) * HEAD)
+            values = total[place, :, cols]
+            if head <= GROUP:
+                values = values * cosine[...] + pltpu.roll(values, HEAD // 2, 1) * sine[...]
+            turned[place, :, cols] = values.astype(BF16)
+        if i < len(others):
+            turned_sends.append(
+                remote(
+                    turned.at[place],
+                    out.at[:, here],
+                    turned_send.at[i],
+                    turned_recv.at[spot],
+                    level * plane + place,
+                    core,
+                )
+            )
+            turned_sends[-1].start()
+    turned_own = pltpu.make_async_copy(turned.at[spot], out.at[:, here], turned_local)
+    turned_own.start()
+
+    for copy in out_sends + slab_sends + normed_sends:
+        copy.wait_send()
+    passed(slab, slab_send, slab_recv)
+
+    @pl.loop(0, depth)
+    def _(target):
+        @pl.when(jnp.logical_not((target == level) & (owner_core == core)))
+        def _():
+            remote(
+                partials.at[target],
+                returned.at[lane, core],
+                partial_send.at[target],
+                partial_recv.at[lane, core],
+                req,
+                sibling,
+            ).wait_send()
+
+    @pl.loop(1, requests)
+    def _(offset):
+        to = (req + offset) % requests
+        remote(
+            outgoing.at[to], arrived.at[req], place_send.at[to], place_recv.at[req], req, sibling
+        ).wait_send()
+
+    for copy in turned_sends:
+        copy.wait_send()
+    turned_own.wait()
+    for other in others:
+        there = pl.ds(pl.multiple_of(other * share, share), share)
+        arrive(out.at[:, there], turned_recv.at[other])
+
+
+def fused_shards(
+    vit_context,
+    vision_residual,
+    out_weight,
+    layer_scale,
+    prompt,
+    prompt_len,
+    image_at,
+    grid_sizes,
+    image_owner,
+    norm_gain,
+    qkv_weight,
+):
+    requests = lax.axis_size("req")
+    cores = lax.axis_size("tp")
+    device_index = lax.axis_index("req")
+    tp_index = lax.axis_index("tp")
+    patches, width = vit_context.shape
+    rows = patches // 4
+    share = (GROUP + 2) * HEAD
+    plane = qkv_weight.shape[1] // share
+    depth = requests // plane
+    seq_slots = prompt.shape[1] + IMG_MAX
+
+    averaging = jnp.where(
+        jnp.arange(patches)[None, :] // 4 == jnp.arange(rows)[:, None], 0.25, 0.0
+    ).astype(BF16)
+    counts, starts = request_plan(grid_sizes, image_owner, requests)
+    request_ends = starts + counts
+    capacity = (IMG_MAX + requests - 1) // requests
+    request_ids = jnp.arange(requests, dtype=jnp.int32)
+    group_index = jnp.arange(rows, dtype=jnp.int32) * requests + device_index
+    destination = jnp.sum((request_ends[None, :] <= group_index[:, None]).astype(jnp.int32), axis=1)
+    owned_start = jnp.sum(
+        jnp.where(destination[:, None] == request_ids[None, :], starts[None, :], 0), axis=1
+    )
+    target = destination * 2 * capacity + (group_index - owned_start) // requests
+    usable = destination < requests
+    slots = jnp.arange(requests * 2 * capacity, dtype=jnp.int32)
+    place_left = ((slots[:, None] == target[None, :]) & usable[None, :]).astype(BF16)
+    place_right = ((slots[:, None] == target[None, :] + capacity) & usable[None, :]).astype(BF16)
+    own_request = request_ids == device_index
+    own_count = jnp.sum(jnp.where(own_request, counts, 0))
+    own_start = jnp.sum(jnp.where(own_request, starts, 0))
+    image_from = image_at[0]
+    prompt_count = prompt_len[0]
+    slot_index = jnp.arange(seq_slots, dtype=jnp.int32)
+    image_row = slot_index - image_from
+    in_image = (image_row >= 0) & (image_row < own_count)
+    is_live = slot_index < prompt_count + own_count
+    from_prompt = is_live & jnp.logical_not(in_image)
+    flat_index = (own_start + image_row) % requests * 2 * capacity + image_row // requests
+    pick_left = ((flat_index[:, None] == slots[None, :]) & in_image[:, None]).astype(BF16)
+    pick_right = ((flat_index[:, None] + capacity == slots[None, :]) & in_image[:, None]).astype(
+        BF16
+    )
+    prompt_row = jnp.where(slot_index < image_from, slot_index, slot_index - own_count)
+    prompt_ids = jnp.arange(prompt.shape[1], dtype=jnp.int32)
+    prompt_pick = ((prompt_row[:, None] == prompt_ids[None, :]) & from_prompt[:, None]).astype(BF16)
+    own_gain = lax.dynamic_slice_in_dim(norm_gain, tp_index * width, width, 0)
+    cosine_table, sine_table = rope_tables(seq_slots)
+    cosine = jnp.concatenate([cosine_table, cosine_table], axis=1)
+    sine = jnp.concatenate([-sine_table, sine_table], axis=1)
+
+    vmem = pl.BlockSpec(memory_space=pltpu.VMEM)
+    anywhere = pl.BlockSpec(memory_space=pl.ANY)
+    dma = pltpu.SemaphoreType.DMA
+    columns = out_weight.shape[1]
+    half = width // 2
+    return pl.pallas_call(
+        functools.partial(fused_kernel, (requests, cores, plane, depth)),
+        out_shape=jax.ShapeDtypeStruct((seq_slots, qkv_weight.shape[1]), BF16),
+        in_specs=[vmem, vmem, anywhere, vmem, vmem, vmem, anywhere] + [vmem] * 8,
+        out_specs=anywhere,
+        scratch_shapes=[
+            pltpu.VMEM((depth, plane, qkv_weight.shape[0], share), BF16),
+            pltpu.VMEM((plane, width, columns), BF16),
+            pltpu.VMEM((depth, rows, width), BF16),
+            pltpu.VMEM((depth, rows, plane * columns), BF16),
+            pltpu.VMEM((depth // cores, cores, rows, plane * columns), BF16),
+            pltpu.VMEM((rows, width), F32),
+            pltpu.VMEM((rows, width), BF16),
+            pltpu.VMEM((requests, 2 * capacity, half), BF16),
+            pltpu.VMEM((requests, 2 * capacity, half), BF16),
+            pltpu.VMEM((seq_slots, width), F32),
+            pltpu.VMEM((2, seq_slots, 128), F32),
+            pltpu.VMEM((plane, cores, seq_slots, width), BF16),
+            pltpu.VMEM((plane, seq_slots, share), F32),
+            pltpu.VMEM((plane, seq_slots, share), BF16),
+            dma((plane,)),
+            dma((plane,)),
+            dma,
+            dma((depth, 2)),
+            dma((depth,)),
+            dma((plane,)),
+            dma((plane,)),
+            dma,
+            dma((depth, 2)),
+            dma((depth,)),
+            dma((depth,)),
+            dma((depth // cores, cores)),
+            dma((requests,)),
+            dma((requests,)),
+            dma,
+            dma,
+            dma((plane,)),
+            dma((plane, cores)),
+            dma((plane,)),
+            dma((plane,)),
+            dma((plane,)),
+            dma,
+        ],
+        compiler_params=pltpu.CompilerParams(
+            collective_id=0, has_side_effects=True, vmem_limit_bytes=58 * 1024 * 1024
+        ),
+        cost_estimate=pl.CostEstimate(
+            flops=30 * 10**9, bytes_accessed=20 * 2**20, transcendentals=0
+        ),
+    )(
+        vit_context,
+        vision_residual,
+        out_weight,
+        layer_scale[None, :],
+        prompt[0],
+        own_gain[None, :],
+        qkv_weight,
+        averaging,
+        place_left,
+        place_right,
+        pick_left,
+        pick_right,
+        prompt_pick,
+        cosine,
+        sine,
+    )
+
+
 def solution(mesh):
+    requests, cores = mesh.shape["req"], mesh.shape["tp"]
+
+    def shards(*arrays):
+        patches, width = arrays[0].shape
+        plane = arrays[-1].shape[1] // ((GROUP + 2) * HEAD)
+        fits = (
+            cores == 2
+            and plane == 4
+            and requests // plane % cores == 0
+            and arrays[2].shape[1] * requests == width * cores
+            and arrays[2].shape[1] % 128 == 0
+            and IMG_MAX % requests == 0
+            and (IMG_MAX // requests) % 8 == 0
+        )
+        return (fused_shards if fits else collective_shards)(*arrays)
+
     in_specs = (
         P("req", "tp"),
         P("req", "tp"),

time: 498 us -> 277 us (0.56)
  waiting for transfers between devices: 325 us -> 0 us
  Pallas kernels: 0 us -> 260 us
  blocking collectives: 75.2 us -> 0 us
  local copies, waits for them, and re-layouts: 28.9 us -> 4.61 us
  matrix products: 23.5 us -> 0 us
  between operations: 15.6 us -> 1.91 us
  starting transfers between devices: 11.7 us -> 0 us
  other arithmetic: 16.6 us -> 9.83 us
    all_gather x5 -> x0, waiting for transfers between devices: 280 us -> none  [the longest x1 116 us: shards(): lax.all_gather(weight_parts.reshape(plane * weight_rows, -1), 'req', axis...]
    pallas_call x0 -> x1, Pallas kernels: none -> 260 us  [fused_shards(): pl.pallas_call(functools.partial(fused_kernel, (requests, cores, plane, d...]
    all_to_all x2 -> x0, blocking collectives: 72.7 us -> none  [the longest x1 40.3 us: shards(): lax.all_to_all(weight_parts, 'req', split_axis=0, concat_axis=0, axis_ind...]
    all_to_all x2 -> x0, waiting for transfers between devices: 37.3 us -> none  [the longest x1 25.7 us: shards(): lax.all_to_all(partial_value.astype(jnp.bfloat16).reshape(depth, merged_c...]
    dot_general x5 -> x0, matrix products: 23.5 us -> none  [the longest x1 14.8 us: shards(): jnp.dot(normed, decoder_weight, preferred_element_type=jnp.float32)]
    reshape x5 -> x0, local copies, waits for them, and re-layouts: 14.8 us -> none  [the longest x1 4.84 us: shards(): vit_context.astype(jnp.float32).reshape(-1, 4, feature_width)]
    all_to_all x2 -> x0, starting transfers between devices: 11.5 us -> none  [the longest x1 6.8 us: shards(): lax.all_to_all(outgoing.reshape(requests, capacity, feature_width), 'req'...]
    reduce_sum x5 -> x3, other arithmetic: 10.7 us -> 0.81 us  [the longest x1 0.63 us: fused_shards(): own_start = jnp.sum(jnp.where(own_request, starts, 0))]
  transfers between devices with their start and end apart: 8 -> 0, of which waited for: 8 -> 0; matrix products, arithmetic and copies ran while one was open for 3% -> 0% of each run, Pallas kernels for 0% -> 0%
where the time goes in v2:
time: 277 us; the launch traced here: 276 us
  Pallas kernels  260 us (94%)
  other arithmetic  9.83 us (4%)
  local copies, waits for them, and re-layouts  4.61 us (2%)
    pallas_call x1, Pallas kernels, fused_shards(): pl.pallas_call(functools.partial(fused_kernel, (requests, cores, plane, d...  260 us

profile of v2, /device:TPU:0, one launch (start us, length us, event | category | flops | bytes accessed | tf_op | source)
XLA Modules:
  0.0 276.3 jit_solution(4752990639928767392)
XLA Ops:
  1.3 0.8 multiply_bitcast_fusion
  2.1 0.8 select_reduce_fusion.1
  2.9 1.3 dynamic_slice.3
  4.2 0.1 copy.14
  4.3 0.1 reduce
  4.4 0.1 convert_reduce_fusion
  4.5 0.6 fusion.26
  5.7 0.1 select_reduce_fusion
  5.8 0.6 fusion.25
  6.4 0.7 broadcast_add_fusion
  7.0 1.2 fusion.15
  8.3 0.7 select_convert_fusion.averaging
  8.9 0.7 fusion.11
  9.6 0.8 fusion.5.prompt_pick
  10.5 1.0 fusion.3
  11.4 0.7 fusion.12
  12.2 0.9 pad_maximum_fusion
  13.1 260.0 %shard_map.109 = bf16[384,3072]{1,0:T(8,128)(2,1)} custom-call(bf16[512,2048]{1,0:T(8,128)(2,1)} %context.1, bf16[512,2048]{1,0:T(8,128)(2,1)} %residual.1, bf16[2048,256]{1,0:T(8,128)(2,1)} %out_weight.1, f32[1,2048]{1,0:T(1,128)} %bitcast.15, bf16[256,2048]{1,0:T(8,128)(2,1)} %bitcast.14, f32[1,2048]{1,0:T(1,128)} %bitcast.12, ...), custom_call_target="tpu_custom_call" | custom-call | flops 30000001024 | bytes 20971520 | tf_op jit(solution)/shard_map/pallas_call | solution.py:660
  273.1 3.2 %copy.18 = bf16[384,3072]{1,0:T(8,128)(2,1)} copy(bf16[384,3072]{1,0:T(8,128)(2,1)} %shard_map.109) | data formatting | bytes 4718592
  (6 shorter events, 0.1 us)

commit v3 on v2

--- a/solution.py
+++ b/solution.py
@@ -193,12 +193,9 @@
     prompt,
     gain,
     qkv_weight,
-    averaging,
-    place_left,
-    place_right,
-    pick_left,
-    pick_right,
-    prompt_pick,
+    target_row,
+    image_from,
+    slot_from,
     cosine,
     sine,
     out,
@@ -211,9 +208,12 @@
     merged,
     outgoing,
     arrived,
-    embedded,
+    images,
     squares,
-    normed,
+    image_squares,
+    texts,
+    pictures,
+    sources,
     total,
     turned,
     slab_in_send,
@@ -232,9 +232,14 @@
     place_recv,
     square_send,
     square_recv,
-    normed_send,
-    normed_recv,
-    cross_send,
+    text_send,
+    text_recv,
+    text_cross,
+    picture_send,
+    picture_recv,
+    picture_cross,
+    source_send,
+    source_recv,
     turned_send,
     turned_recv,
     turned_local,
@@ -298,9 +303,13 @@
     out_own = pltpu.make_async_copy(out_weight, out_slab.at[spot], out_slab_local)
     out_own.start()
 
+    first_patch = 4 * lax.broadcasted_iota(jnp.int32, (rows, 4 * rows), 0)
+    patch = lax.broadcasted_iota(jnp.int32, (rows, 4 * rows), 1)
+    inside = (patch >= first_patch) & (patch < first_patch + 4)
+    averaging = jnp.where(inside, 0.25, 0.0).astype(BF16)
     for i in range(width // 512):
         cols = slice(i * 512, (i + 1) * 512)
-        blocks[level, :, cols] = dot(averaging[...], context[:, cols]).astype(BF16)
+        blocks[level, :, cols] = dot(averaging, context[:, cols]).astype(BF16)
 
     def pass_on(buffer, send, recv, hop, first):
         if hop > 1:
@@ -372,7 +381,32 @@
 
     for i in range(width // 512):
         cols = slice(i * 512, (i + 1) * 512)
-        mean_residual[:, cols] = dot(averaging[...], residual[:, cols])
+        mean_residual[:, cols] = dot(averaging, residual[:, cols])
+
+    own_gain = gain[:, pl.ds(pl.multiple_of(core * width, width), width)]
+
+    def squares_of(values):
+        return jnp.broadcast_to(
+            jnp.sum(values * values, axis=-1, keepdims=True), (values.shape[0], 128)
+        )
+
+    def share_squares(buffer, i):
+        copy = remote(
+            buffer.at[0], buffer.at[1], square_send.at[i], square_recv.at[i], req, sibling
+        )
+        copy.start()
+        copy.wait()
+        mean_square = (buffer[0, :, :1] + buffer[1, :, :1]) / (width * cores)
+        return lax.rsqrt(mean_square + 1e-05)
+
+    squares[0] = squares_of(prompt[...].astype(F32))
+    factor = share_squares(squares, 0)
+    for i in range(width // 512):
+        cols = slice(i * 512, (i + 1) * 512)
+        texts[spot, core, :, cols] = (
+            prompt[:, cols].astype(F32) * factor * own_gain[:, cols]
+        ).astype(BF16)
+    sources[spot] = jnp.broadcast_to(slot_from[...], sources.shape[1:]).astype(BF16)
 
     for hop in range(2, depth + 1):
         pass_on(blocks, block_send, block_recv, hop, True)
@@ -386,6 +420,34 @@
     out_own.wait()
     for other in others:
         arrive(out_slab.at[other], out_slab_recv.at[other])
+
+    def spread(buffer, send, recv):
+        copies = []
+        for i, other in enumerate(others):
+            own = buffer.at[spot, core]
+            copies.append(
+                remote(own, own, send.at[i], recv.at[spot, core], level * plane + other, core)
+            )
+            copies[-1].start()
+        return copies
+
+    def cross(buffer, place, send, recv):
+        part = buffer.at[place, core]
+        copy = remote(part, part, send, recv.at[place, core], req, sibling)
+        copy.start()
+        return copy
+
+    sends = []
+    for i, other in enumerate(others):
+        own = sources.at[spot]
+        sends.append(
+            remote(
+                own, own, source_send.at[i], source_recv.at[spot], level * plane + other, core
+            )
+        )
+        sends[-1].start()
+    sends.extend(spread(texts, text_send, text_recv))
+    sends.append(cross(texts, spot, text_cross.at[0], text_recv))
 
     owner_core = level // held
     lane = level % held
@@ -426,7 +488,12 @@
             added = added + returned[i, j].astype(F32)
         merged[:, cols] = (mean_residual[:, cols] + scale[:, cols] * added).astype(BF16)
 
-    placed = dot(place_left[...], merged[:, :half]) + dot(place_right[...], merged[:, half:])
+    block_rows = outgoing.shape[1]
+    slot = lax.broadcasted_iota(jnp.int32, (requests * block_rows, rows), 0)
+    placed = jnp.zeros((requests * block_rows, half), F32)
+    for i in range(2):
+        place = jnp.where(slot == target_row[...] + i * (block_rows // 2), 1.0, 0.0).astype(BF16)
+        placed = placed + dot(place, merged[:, i * half : (i + 1) * half])
     outgoing[...] = placed.astype(BF16).reshape(outgoing.shape)
 
     @pl.loop(1, requests)
@@ -438,9 +505,7 @@
 
     place_own = pltpu.make_async_copy(outgoing.at[req], arrived.at[req], place_send.at[req])
     place_own.start()
-    for i in range(2):
-        cols = slice(i * half, (i + 1) * half)
-        embedded[:, cols] = dot(prompt_pick[...], prompt[:, cols])
+    pass_on(slab, slab_send, slab_recv, 2, False)
     place_own.wait()
 
     @pl.loop(1, requests)
@@ -448,115 +513,110 @@
         source = (req + offset) % requests
         arrive(arrived.at[source], place_recv.at[source])
 
-    square_sum = jnp.zeros((seq, 1), F32)
-    for i, pick in enumerate((pick_left, pick_right)):
-        cols = slice(i * half, (i + 1) * half)
-        images = arrived[...].reshape(arrived.shape[0] * arrived.shape[1], half)
-        values = embedded[:, cols] + dot(pick[...], images)
-        embedded[:, cols] = values
-        square_sum = square_sum + jnp.sum(values * values, axis=-1, keepdims=True)
-    squares[0] = jnp.broadcast_to(square_sum, squares.shape[1:])
-    square_copy = remote(squares.at[0], squares.at[1], square_send, square_recv, req, sibling)
-    square_copy.start()
-    square_copy.wait()
-    mean_square = (squares[0, :, :1] + squares[1, :, :1]) / (width * cores)
-    factor = lax.rsqrt(mean_square + 1e-05)
+    slot = lax.broadcasted_iota(jnp.int32, (images.shape[0], requests * block_rows), 1)
+    for i in range(2):
+        pick = jnp.where(slot == image_from[...] + i * (block_rows // 2), 1.0, 0.0).astype(BF16)
+        images[:, i * half : (i + 1) * half] = dot(
+            pick, arrived[...].reshape(requests * block_rows, half)
+        )
+    image_squares[0] = squares_of(images[...])
+    factor = share_squares(image_squares, 1)
     for i in range(2):
         cols = slice(i * half, (i + 1) * half)
-        normed[spot, core, :, cols] = (embedded[:, cols] * factor * gain[:, cols]).astype(BF16)
-
-    normed_sends = []
+        pictures[spot, core, :, cols] = (images[:, cols] * factor * own_gain[:, cols]).astype(BF16)
+    sends.extend(spread(pictures, picture_send, picture_recv))
+    sends.append(cross(pictures, spot, picture_cross.at[0], picture_recv))
+
     for i, other in enumerate(others):
-        normed_sends.append(
-            remote(
-                normed.at[spot, core],
-                normed.at[spot, core],
-                normed_send.at[i],
-                normed_recv.at[spot, core],
-                level * plane + other,
-                core,
-            )
-        )
-        normed_sends[-1].start()
-
-    def cross(place, i):
-        copy = remote(
-            normed.at[place, core],
-            normed.at[place, core],
-            cross_send.at[i],
-            normed_recv.at[place, core],
-            req,
-            sibling,
-        )
-        copy.start()
-        normed_sends.append(copy)
-
-    cross(spot, 0)
-    pass_on(slab, slab_send, slab_recv, 2, False)
+        arrive(texts.at[other, core], text_recv.at[other, core])
+        sends.append(cross(texts, other, text_cross.at[i + 1], text_recv))
+        arrive(sources.at[other], source_recv.at[other])
+    for i, other in enumerate(others):
+        arrive(pictures.at[other, core], picture_recv.at[other, core])
+        sends.append(cross(pictures, other, picture_cross.at[i + 1], picture_recv))
     for hop in range(3, depth):
         pass_on(slab, slab_send, slab_recv, hop, False)
-    for i, other in enumerate(others):
-        arrive(normed.at[other, core], normed_recv.at[other, core])
-        cross(other, i + 1)
     for place in [spot] + others:
-        arrive(normed.at[place, sibling], normed_recv.at[place, sibling])
+        arrive(texts.at[place, sibling], text_recv.at[place, sibling])
+        arrive(pictures.at[place, sibling], picture_recv.at[place, sibling])
 
     tile = 256
     level_rows = plane * depth_rows
-
-    def multiply(at, first):
+    seq_texts = texts.shape[2]
+    lanes = lax.broadcasted_iota(jnp.int32, (seq, 128), 1).astype(F32)
+
+    def multiply(at, place, first):
         part = at // held
         base = pl.multiple_of((at % held) * level_rows, level_rows)
-
+        source = sources[place].astype(F32)
+        picks = [
+            jnp.where(source == lanes + i * 128, 1.0, 0.0).astype(BF16)
+            for i in range(seq_texts // 128)
+        ]
+        image_pick = jnp.where(source == -1.0 - lanes, 1.0, 0.0).astype(BF16)
+        text_pick = jnp.concatenate(picks, axis=1)
+        a = dot(text_pick, texts[place, part, :, pl.ds(base, level_rows)]) + dot(
+            image_pick, pictures[place, part, :, pl.ds(base, level_rows)]
+        )
+        a = a.astype(BF16)
+        for n in range(share // tile):
+            cols = slice(n * tile, (n + 1) * tile)
+            b = slab[at, :, :, cols].reshape(level_rows, tile)
+            if first:
+                total[place, :, cols] = dot(a, b)
+            else:
+                total[place, :, cols] += dot(a, b)
+
+    def multiply_all(at, first):
         @pl.loop(0, plane)
         def _(place):
-            a = normed[place, part, :, pl.ds(base, level_rows)]
-            for n in range(share // tile):
-                cols = slice(n * tile, (n + 1) * tile)
-                b = slab[at, :, :, cols].reshape(level_rows, tile)
-                if first:
-                    total[place, :, cols] = dot(a, b)
-                else:
-                    total[place, :, cols] += dot(a, b)
-
-    multiply(level, True)
-    for hop in range(1, depth):
-        if hop == depth - 1:
-            pass_on(slab, slab_send, slab_recv, depth, False)
+            multiply(at, place, first)
+
+    multiply_all(level, True)
+    for hop in range(1, depth - 1):
 
         @pl.when(level - hop >= 0)
         def _():
-            multiply(level - hop, False)
+            multiply_all(level - hop, False)
 
         @pl.when(level + hop < depth)
         def _():
-            multiply(level + hop, False)
-
-    turned_sends = []
+            multiply_all(level + hop, False)
+
+    pass_on(slab, slab_send, slab_recv, depth, False)
+    last = depth - 1 - level
     here = pl.ds(pl.multiple_of(spot * share, share), share)
-    for i, place in enumerate(others + [spot]):
+
+    @pl.loop(0, plane)
+    def _(step):
+        place = (spot + 1 + step) % plane
+
+        @pl.when((level == 0) | (level == depth - 1))
+        def _():
+            multiply(last, place, False)
+
         for head in range(share // HEAD):
             cols = slice(head * HEAD, (head + 1) * HEAD)
             values = total[place, :, cols]
             if head <= GROUP:
                 values = values * cosine[...] + pltpu.roll(values, HEAD // 2, 1) * sine[...]
             turned[place, :, cols] = values.astype(BF16)
-        if i < len(others):
-            turned_sends.append(
-                remote(
-                    turned.at[place],
-                    out.at[:, here],
-                    turned_send.at[i],
-                    turned_recv.at[spot],
-                    level * plane + place,
-                    core,
-                )
-            )
-            turned_sends[-1].start()
+
+        @pl.when(step < plane - 1)
+        def _():
+            remote(
+                turned.at[place],
+                out.at[:, here],
+                turned_send.at[place],
+                turned_recv.at[spot],
+                level * plane + place,
+                core,
+            ).start()
+
     turned_own = pltpu.make_async_copy(turned.at[spot], out.at[:, here], turned_local)
     turned_own.start()
 
-    for copy in out_sends + slab_sends + normed_sends:
+    for copy in out_sends + slab_sends + sends:
         copy.wait_send()
     passed(slab, slab_send, slab_recv)
 
@@ -580,8 +640,15 @@
             outgoing.at[to], arrived.at[req], place_send.at[to], place_recv.at[req], req, sibling
         ).wait_send()
 
-    for copy in turned_sends:
-        copy.wait_send()
+    for other in others:
+        remote(
+            turned.at[other],
+            out.at[:, here],
+            turned_send.at[other],
+            turned_recv.at[spot],
+            req,
+            sibling,
+        ).wait_send()
     turned_own.wait()
     for other in others:
         there = pl.ds(pl.multiple_of(other * share, share), share)
@@ -612,9 +679,6 @@
     depth = requests // plane
     seq_slots = prompt.shape[1] + IMG_MAX
 
-    averaging = jnp.where(
-        jnp.arange(patches)[None, :] // 4 == jnp.arange(rows)[:, None], 0.25, 0.0
-    ).astype(BF16)
     counts, starts = request_plan(grid_sizes, image_owner, requests)
     request_ends = starts + counts
     capacity = (IMG_MAX + requests - 1) // requests
@@ -626,28 +690,21 @@
     )
     target = destination * 2 * capacity + (group_index - owned_start) // requests
     usable = destination < requests
-    slots = jnp.arange(requests * 2 * capacity, dtype=jnp.int32)
-    place_left = ((slots[:, None] == target[None, :]) & usable[None, :]).astype(BF16)
-    place_right = ((slots[:, None] == target[None, :] + capacity) & usable[None, :]).astype(BF16)
+    target = jnp.where(usable, target, -requests * 2 * capacity)
     own_request = request_ids == device_index
     own_count = jnp.sum(jnp.where(own_request, counts, 0))
     own_start = jnp.sum(jnp.where(own_request, starts, 0))
     image_from = image_at[0]
     prompt_count = prompt_len[0]
+    image_row = jnp.arange(IMG_MAX, dtype=jnp.int32)
+    from_flat = (own_start + image_row) % requests * 2 * capacity + image_row // requests
+    from_flat = jnp.where(image_row < own_count, from_flat, -requests * 2 * capacity)
     slot_index = jnp.arange(seq_slots, dtype=jnp.int32)
-    image_row = slot_index - image_from
-    in_image = (image_row >= 0) & (image_row < own_count)
-    is_live = slot_index < prompt_count + own_count
-    from_prompt = is_live & jnp.logical_not(in_image)
-    flat_index = (own_start + image_row) % requests * 2 * capacity + image_row // requests
-    pick_left = ((flat_index[:, None] == slots[None, :]) & in_image[:, None]).astype(BF16)
-    pick_right = ((flat_index[:, None] + capacity == slots[None, :]) & in_image[:, None]).astype(
-        BF16
-    )
-    prompt_row = jnp.where(slot_index < image_from, slot_index, slot_index - own_count)
-    prompt_ids = jnp.arange(prompt.shape[1], dtype=jnp.int32)
-    prompt_pick = ((prompt_row[:, None] == prompt_ids[None, :]) & from_prompt[:, None]).astype(BF16)
-    own_gain = lax.dynamic_slice_in_dim(norm_gain, tp_index * width, width, 0)
+    slot_image = slot_index - image_from
+    in_image = (slot_image >= 0) & (slot_image < own_count)
+    slot_row = jnp.where(slot_index < image_from, slot_index, slot_index - own_count)
+    slot_from = jnp.where(slot_index < prompt_count + own_count, slot_row, 512)
+    slot_from = jnp.where(in_image, -1 - slot_image, slot_from)
     cosine_table, sine_table = rope_tables(seq_slots)
     cosine = jnp.concatenate([cosine_table, cosine_table], axis=1)
     sine = jnp.concatenate([-sine_table, sine_table], axis=1)
@@ -660,7 +717,7 @@
     return pl.pallas_call(
         functools.partial(fused_kernel, (requests, cores, plane, depth)),
         out_shape=jax.ShapeDtypeStruct((seq_slots, qkv_weight.shape[1]), BF16),
-        in_specs=[vmem, vmem, anywhere, vmem, vmem, vmem, anywhere] + [vmem] * 8,
+        in_specs=[vmem, vmem, anywhere, vmem, vmem, vmem, anywhere] + [vmem] * 5,
         out_specs=anywhere,
         scratch_shapes=[
             pltpu.VMEM((depth, plane, qkv_weight.shape[0], share), BF16),
@@ -672,9 +729,12 @@
             pltpu.VMEM((rows, width), BF16),
             pltpu.VMEM((requests, 2 * capacity, half), BF16),
             pltpu.VMEM((requests, 2 * capacity, half), BF16),
-            pltpu.VMEM((seq_slots, width), F32),
-            pltpu.VMEM((2, seq_slots, 128), F32),
-            pltpu.VMEM((plane, cores, seq_slots, width), BF16),
+            pltpu.VMEM((IMG_MAX, width), F32),
+            pltpu.VMEM((2, prompt.shape[1], 128), F32),
+            pltpu.VMEM((2, IMG_MAX, 128), F32),
+            pltpu.VMEM((plane, cores, prompt.shape[1], width), BF16),
+            pltpu.VMEM((plane, cores, IMG_MAX, width), BF16),
+            pltpu.VMEM((plane, seq_slots, 128), BF16),
             pltpu.VMEM((plane, seq_slots, share), F32),
             pltpu.VMEM((plane, seq_slots, share), BF16),
             dma((plane,)),
@@ -691,10 +751,15 @@
             dma((depth // cores, cores)),
             dma((requests,)),
             dma((requests,)),
-            dma,
-            dma,
+            dma((2,)),
+            dma((2,)),
             dma((plane,)),
             dma((plane, cores)),
+            dma((plane,)),
+            dma((plane,)),
+            dma((plane, cores)),
+            dma((plane,)),
+            dma((plane,)),
             dma((plane,)),
             dma((plane,)),
             dma((plane,)),
@@ -712,14 +777,11 @@
         out_weight,
         layer_scale[None, :],
         prompt[0],
-        own_gain[None, :],
+        norm_gain[None, :],
         qkv_weight,
-        averaging,
-        place_left,
-        place_right,
-        pick_left,
-        pick_right,
-        prompt_pick,
+        target[None, :],
+        from_flat[:, None],
+        slot_from[:, None],
         cosine,
         sine,
     )
@@ -739,6 +801,8 @@
             and arrays[2].shape[1] % 128 == 0
             and IMG_MAX % requests == 0
             and (IMG_MAX // requests) % 8 == 0
+            and IMG_MAX == 128
+            and arrays[4].shape[1] in (128, 256)
         )
         return (fused_shards if fits else collective_shards)(*arrays)
 

time: 277 us -> 253 us (0.913)
  Pallas kernels: 260 us -> 240 us
    pallas_call x1, Pallas kernels: 260 us -> 240 us  [fused_shards(): pl.pallas_call(functools.partial(fused_kernel, (requests, cores, plane, d...]
    select_n x1 -> x3, other arithmetic: 0.01 us -> 3.74 us  [the longest x1 1.86 us: fused_shards(): jnp.where(image_row < own_count, from_flat, -requests * 2 * capacity)]
    convert_element_type x4 -> x0, other arithmetic: 3.17 us -> none  [the longest x1 0.95 us: fused_shards(): ((flat_index[:, None] + capacity == slots[None, :]) & in_image[:, None])....]
where the time goes in v3:
time: 253 us
  Pallas kernels  240 us (95%)
  other arithmetic  7.91 us (3%)
  local copies, waits for them, and re-layouts  3.31 us (1%)
    pallas_call x1, Pallas kernels, fused_shards(): pl.pallas_call(functools.partial(fused_kernel, (requests, cores, plane, d...  240 us

profile of v3, /device:TPU:0, one launch (start us, length us, event | category | flops | bytes accessed | tf_op | source)
XLA Modules:
  0.0 252.8 jit_solution(9800596295189469468)
XLA Ops:
  1.3 0.8 multiply_bitcast_fusion
  2.1 0.8 select_reduce_fusion.1
  2.8 0.1 copy.14
  3.0 0.1 reduce
  3.1 0.1 convert_reduce_fusion
  3.2 0.6 fusion.17
  4.4 0.1 select_reduce_fusion
  4.5 0.6 bitcast_select_fusion.target_row
  5.0 1.9 fusion.9.image_from
  6.9 1.3 select_select_fusion.slot_from
  8.2 0.7 fusion.5
  9.0 0.9 pad_maximum_fusion
  9.9 239.7 %shard_map.109 = bf16[384,3072]{1,0:T(8,128)(2,1)} custom-call(bf16[512,2048]{1,0:T(8,128)(2,1)} %context.1, bf16[512,2048]{1,0:T(8,128)(2,1)} %residual.1, bf16[2048,256]{1,0:T(8,128)(2,1)} %out_weight.1, f32[1,2048]{1,0:T(1,128)} %bitcast.23, bf16[256,2048]{1,0:T(8,128)(2,1)} %bitcast.21, f32[1,4096]{1,0:T(1,128)} %bitcast.22, ...), custom_call_target="tpu_custom_call" | custom-call | flops 30000001024 | bytes 20971520 | tf_op jit(solution)/shard_map/pallas_call | solution.py:717
  249.6 3.2 %copy.18 = bf16[384,3072]{1,0:T(8,128)(2,1)} copy(bf16[384,3072]{1,0:T(8,128)(2,1)} %shard_map.109) | data formatting | bytes 4718592
  (3 shorter events, 0.1 us)

commit v4 on v3

--- a/solution.py
+++ b/solution.py
@@ -216,6 +216,7 @@
     sources,
     total,
     turned,
+    assembled,
     slab_in_send,
     slab_in_recv,
     slab_local,
@@ -243,6 +244,10 @@
     turned_send,
     turned_recv,
     turned_local,
+    slab_far_send,
+    slab_far_recv,
+    block_far_send,
+    block_far_recv,
 ):
     requests, cores, plane, depth = dims
     req = lax.axis_index("req")
@@ -287,77 +292,6 @@
 
     pl.semaphore_wait(barrier, count - 1)
 
-    out_sends = []
-    for i, other in enumerate(others):
-        out_sends.append(
-            remote(
-                out_weight,
-                out_slab.at[spot],
-                out_slab_send.at[i],
-                out_slab_recv.at[spot],
-                level * plane + other,
-                core,
-            )
-        )
-        out_sends[-1].start()
-    out_own = pltpu.make_async_copy(out_weight, out_slab.at[spot], out_slab_local)
-    out_own.start()
-
-    first_patch = 4 * lax.broadcasted_iota(jnp.int32, (rows, 4 * rows), 0)
-    patch = lax.broadcasted_iota(jnp.int32, (rows, 4 * rows), 1)
-    inside = (patch >= first_patch) & (patch < first_patch + 4)
-    averaging = jnp.where(inside, 0.25, 0.0).astype(BF16)
-    for i in range(width // 512):
-        cols = slice(i * 512, (i + 1) * 512)
-        blocks[level, :, cols] = dot(averaging, context[:, cols]).astype(BF16)
-
-    def pass_on(buffer, send, recv, hop, first):
-        if hop > 1:
-
-            @pl.when(level - (hop - 1) >= 0)
-            def _():
-                arrive(buffer.at[level - (hop - 1)], recv.at[level - (hop - 1)])
-
-            @pl.when(level + (hop - 1) < depth)
-            def _():
-                arrive(buffer.at[level + (hop - 1)], recv.at[level + (hop - 1)])
-
-        if hop == depth:
-            return
-
-        @pl.when((level - (hop - 1) >= 0) & (level + 1 < depth))
-        def _():
-            at = level - (hop - 1)
-            remote(
-                buffer.at[at], buffer.at[at], send.at[hop - 1, 0], recv.at[at], req + plane, core
-            ).start()
-
-        @pl.when((level + (hop - 1) < depth) & (level - 1 >= 0))
-        def _():
-            at = level + (hop - 1)
-            remote(
-                buffer.at[at], buffer.at[at], send.at[hop - 1, 1], recv.at[at], req - plane, core
-            ).start()
-
-    def passed(buffer, send, recv):
-        for hop in range(1, depth):
-
-            @pl.when((level - (hop - 1) >= 0) & (level + 1 < depth))
-            def _():
-                at = level - (hop - 1)
-                remote(
-                    buffer.at[at], buffer.at[at], send.at[hop - 1, 0], recv.at[at], req, sibling
-                ).wait_send()
-
-            @pl.when((level + (hop - 1) < depth) & (level - 1 >= 0))
-            def _():
-                at = level + (hop - 1)
-                remote(
-                    buffer.at[at], buffer.at[at], send.at[hop - 1, 1], recv.at[at], req, sibling
-                ).wait_send()
-
-    pass_on(blocks, block_send, block_recv, 1, True)
-
     slab_sends = []
     for i, other in enumerate(others):
         at = pl.multiple_of(other * share, share)
@@ -379,6 +313,90 @@
     )
     slab_own.start()
 
+    out_sends = []
+    for i, other in enumerate(others):
+        out_sends.append(
+            remote(
+                out_weight,
+                out_slab.at[spot],
+                out_slab_send.at[i],
+                out_slab_recv.at[spot],
+                level * plane + other,
+                core,
+            )
+        )
+        out_sends[-1].start()
+    out_own = pltpu.make_async_copy(out_weight, out_slab.at[spot], out_slab_local)
+    out_own.start()
+
+    first_patch = 4 * lax.broadcasted_iota(jnp.int32, (rows, 4 * rows), 0)
+    patch = lax.broadcasted_iota(jnp.int32, (rows, 4 * rows), 1)
+    inside = (patch >= first_patch) & (patch < first_patch + 4)
+    averaging = jnp.where(inside, 0.25, 0.0).astype(BF16)
+    for i in range(width // 512):
+        cols = slice(i * 512, (i + 1) * 512)
+        blocks[level, :, cols] = dot(averaging, context[:, cols]).astype(BF16)
+
+    def hand(part, send, recv, to_level):
+        return remote(part, part, send, recv, to_level * plane + spot, core)
+
+    def near_copies(buffer, send, recv):
+        own = buffer.at[level]
+        for d in (1, 2):
+            yield level + d < depth, hand(own, send.at[d - 1, 0], recv.at[level], level + d)
+            yield level - d >= 0, hand(own, send.at[d - 1, 1], recv.at[level], level - d)
+
+    def near_start(buffer, send, recv):
+        for there, copy in near_copies(buffer, send, recv):
+            pl.when(there)(copy.start)
+
+    def near_sent(buffer, send, recv):
+        for there, copy in near_copies(buffer, send, recv):
+            pl.when(there)(copy.wait_send)
+
+    def far_copies(buffer, send, far_recv):
+        pieces = far_recv.shape[0]
+        size = buffer.shape[-1] // pieces
+        for here, at, to in ((2, 0, 3), (1, 3, 0)):
+            for i in range(pieces):
+                part = buffer.at[at, ..., pl.ds(i * size, size)]
+                yield level == here, hand(part, send.at[i], far_recv.at[i], to)
+
+    def far_start(buffer, recv, send, far_recv):
+        @pl.when(level == 2)
+        def _():
+            arrive(buffer.at[0], recv.at[0])
+
+        @pl.when(level == 1)
+        def _():
+            arrive(buffer.at[3], recv.at[3])
+
+        for there, copy in far_copies(buffer, send, far_recv):
+            pl.when(there)(copy.start)
+
+    def far_sent(buffer, send, far_recv):
+        for there, copy in far_copies(buffer, send, far_recv):
+            pl.when(there)(copy.wait_send)
+
+    def near_arrive(buffer, recv, d):
+        @pl.when((level - d >= 0) & ((d == 1) | (level == 3)))
+        def _():
+            arrive(buffer.at[level - d], recv.at[level - d])
+
+        @pl.when((level + d < depth) & ((d == 1) | (level == 0)))
+        def _():
+            arrive(buffer.at[level + d], recv.at[level + d])
+
+    def far_arrive(buffer, far_recv, i):
+        size = buffer.shape[-1] // far_recv.shape[0]
+        for here, at in ((0, 3), (3, 0)):
+
+            @pl.when(level == here)
+            def _():
+                arrive(buffer.at[at, ..., pl.ds(i * size, size)], far_recv.at[i])
+
+    near_start(blocks, block_send, block_recv)
+
     for i in range(width // 512):
         cols = slice(i * 512, (i + 1) * 512)
         mean_residual[:, cols] = dot(averaging, residual[:, cols])
@@ -408,14 +426,15 @@
         ).astype(BF16)
     sources[spot] = jnp.broadcast_to(slot_from[...], sources.shape[1:]).astype(BF16)
 
-    for hop in range(2, depth + 1):
-        pass_on(blocks, block_send, block_recv, hop, True)
-    passed(blocks, block_send, block_recv)
+    far_start(blocks, block_recv, block_far_send, block_far_recv)
+    near_arrive(blocks, block_recv, 1)
+    near_arrive(blocks, block_recv, 2)
+    far_arrive(blocks, block_far_recv, 0)
 
     slab_own.wait()
     for other in others:
         arrive(slab.at[level, other], slab_in_recv.at[other])
-    pass_on(slab, slab_send, slab_recv, 1, False)
+    near_start(slab, slab_send, slab_recv)
 
     out_own.wait()
     for other in others:
@@ -505,7 +524,6 @@
 
     place_own = pltpu.make_async_copy(outgoing.at[req], arrived.at[req], place_send.at[req])
     place_own.start()
-    pass_on(slab, slab_send, slab_recv, 2, False)
     place_own.wait()
 
     @pl.loop(1, requests)
@@ -526,6 +544,7 @@
         pictures[spot, core, :, cols] = (images[:, cols] * factor * own_gain[:, cols]).astype(BF16)
     sends.extend(spread(pictures, picture_send, picture_recv))
     sends.append(cross(pictures, spot, picture_cross.at[0], picture_recv))
+    far_start(slab, slab_recv, slab_far_send, slab_far_recv)
 
     for i, other in enumerate(others):
         arrive(texts.at[other, core], text_recv.at[other, core])
@@ -534,8 +553,6 @@
     for i, other in enumerate(others):
         arrive(pictures.at[other, core], picture_recv.at[other, core])
         sends.append(cross(pictures, other, picture_cross.at[i + 1], picture_recv))
-    for hop in range(3, depth):
-        pass_on(slab, slab_send, slab_recv, hop, False)
     for place in [spot] + others:
         arrive(texts.at[place, sibling], text_recv.at[place, sibling])
         arrive(pictures.at[place, sibling], picture_recv.at[place, sibling])
@@ -545,7 +562,7 @@
     seq_texts = texts.shape[2]
     lanes = lax.broadcasted_iota(jnp.int32, (seq, 128), 1).astype(F32)
 
-    def multiply(at, place, first):
+    def level_of(at, place):
         part = at // held
         base = pl.multiple_of((at % held) * level_rows, level_rows)
         source = sources[place].astype(F32)
@@ -558,67 +575,86 @@
         a = dot(text_pick, texts[place, part, :, pl.ds(base, level_rows)]) + dot(
             image_pick, pictures[place, part, :, pl.ds(base, level_rows)]
         )
-        a = a.astype(BF16)
-        for n in range(share // tile):
-            cols = slice(n * tile, (n + 1) * tile)
-            b = slab[at, :, :, cols].reshape(level_rows, tile)
-            if first:
-                total[place, :, cols] = dot(a, b)
-            else:
-                total[place, :, cols] += dot(a, b)
+        return a.astype(BF16)
 
     def multiply_all(at, first):
         @pl.loop(0, plane)
         def _(place):
-            multiply(at, place, first)
+            a = level_of(at, place)
+            for n in range(share // tile):
+                cols = slice(n * tile, (n + 1) * tile)
+                b = slab[at, :, :, cols].reshape(level_rows, tile)
+                if first:
+                    total[place, :, cols] = dot(a, b)
+                else:
+                    total[place, :, cols] += dot(a, b)
 
     multiply_all(level, True)
-    for hop in range(1, depth - 1):
-
-        @pl.when(level - hop >= 0)
+    for d in (1, 2):
+        near_arrive(slab, slab_recv, d)
+
+        @pl.when(level - d >= 0)
         def _():
-            multiply_all(level - hop, False)
-
-        @pl.when(level + hop < depth)
+            multiply_all(level - d, False)
+
+        @pl.when(level + d < depth)
         def _():
-            multiply_all(level + hop, False)
-
-    pass_on(slab, slab_send, slab_recv, depth, False)
+            multiply_all(level + d, False)
+
+    at_edge = (level == 0) | (level == depth - 1)
     last = depth - 1 - level
+
+    @pl.when(at_edge)
+    def _():
+        @pl.loop(0, plane)
+        def _(place):
+            assembled[place] = level_of(last, place)
+
+    def leave(place, n):
+        start = pl.multiple_of(spot * share + n * tile, tile)
+        return remote(
+            turned.at[place, :, pl.ds(n * tile, tile)],
+            out.at[:, pl.ds(start, tile)],
+            turned_send.at[place, n],
+            turned_recv.at[spot, n],
+            level * plane + place,
+            core,
+        )
+
+    for n in range(share // tile):
+        far_arrive(slab, slab_far_recv, n)
+
+        @pl.loop(0, plane)
+        def _(step):
+            place = (spot + 1 + step) % plane
+
+            @pl.when(at_edge)
+            def _():
+                cols = slice(n * tile, (n + 1) * tile)
+                b = slab[last, :, :, cols].reshape(level_rows, tile)
+                total[place, :, cols] += dot(assembled[place], b)
+
+            for head in range(n * tile // HEAD, (n + 1) * tile // HEAD):
+                cols = slice(head * HEAD, (head + 1) * HEAD)
+                values = total[place, :, cols]
+                if head <= GROUP:
+                    values = values * cosine[...] + pltpu.roll(values, HEAD // 2, 1) * sine[...]
+                turned[place, :, cols] = values.astype(BF16)
+
+            @pl.when(step < plane - 1)
+            def _():
+                leave(place, n).start()
+
     here = pl.ds(pl.multiple_of(spot * share, share), share)
-
-    @pl.loop(0, plane)
-    def _(step):
-        place = (spot + 1 + step) % plane
-
-        @pl.when((level == 0) | (level == depth - 1))
-        def _():
-            multiply(last, place, False)
-
-        for head in range(share // HEAD):
-            cols = slice(head * HEAD, (head + 1) * HEAD)
-            values = total[place, :, cols]
-            if head <= GROUP:
-                values = values * cosine[...] + pltpu.roll(values, HEAD // 2, 1) * sine[...]
-            turned[place, :, cols] = values.astype(BF16)
-
-        @pl.when(step < plane - 1)
-        def _():
-            remote(
-                turned.at[place],
-                out.at[:, here],
-                turned_send.at[place],
-                turned_recv.at[spot],
-                level * plane + place,
-                core,
-            ).start()
-
     turned_own = pltpu.make_async_copy(turned.at[spot], out.at[:, here], turned_local)
     turned_own.start()
 
     for copy in out_sends + slab_sends + sends:
         copy.wait_send()
-    passed(slab, slab_send, slab_recv)
+    near_sent(blocks, block_send, block_recv)
+    far_sent(blocks, block_far_send, block_far_recv)
+    near_sent(slab, slab_send, slab_recv)
+    far_sent(slab, slab_far_send, slab_far_recv)
 
     @pl.loop(0, depth)
     def _(target):
@@ -641,18 +677,13 @@
         ).wait_send()
 
     for other in others:
-        remote(
-            turned.at[other],
-            out.at[:, here],
-            turned_send.at[other],
-            turned_recv.at[spot],
-            req,
-            sibling,
-        ).wait_send()
+        for n in range(share // tile):
+            leave(other, n).wait_send()
     turned_own.wait()
     for other in others:
-        there = pl.ds(pl.multiple_of(other * share, share), share)
-        arrive(out.at[:, there], turned_recv.at[other])
+        for n in range(share // tile):
+            start = pl.multiple_of(other * share + n * tile, tile)
+            arrive(out.at[:, pl.ds(start, tile)], turned_recv.at[other, n])
 
 
 def fused_shards(
@@ -737,6 +768,7 @@
             pltpu.VMEM((plane, seq_slots, 128), BF16),
             pltpu.VMEM((plane, seq_slots, share), F32),
             pltpu.VMEM((plane, seq_slots, share), BF16),
+            pltpu.VMEM((plane, seq_slots, plane * qkv_weight.shape[0]), BF16),
             dma((plane,)),
             dma((plane,)),
             dma,
@@ -761,9 +793,13 @@
             dma((plane,)),
             dma((plane,)),
             dma((plane,)),
-            dma((plane,)),
-            dma((plane,)),
+            dma((plane, 3)),
+            dma((plane, 3)),
             dma,
+            dma((3,)),
+            dma((3,)),
+            dma((1,)),
+            dma((1,)),
         ],
         compiler_params=pltpu.CompilerParams(
             collective_id=0, has_side_effects=True, vmem_limit_bytes=58 * 1024 * 1024
@@ -796,7 +832,7 @@
         fits = (
             cores == 2
             and plane == 4
-            and requests // plane % cores == 0
+            and requests // plane == 4
             and arrays[2].shape[1] * requests == width * cores
             and arrays[2].shape[1] % 128 == 0
             and IMG_MAX % requests == 0

time: 253 us -> 274 us (1.083)
  Pallas kernels: 240 us -> 258 us
    pallas_call x1, Pallas kernels: 240 us -> 258 us  [fused_shards(): pl.pallas_call(functools.partial(fused_kernel, (requests, cores, plane, d...]
where the time goes in v4:
time: 274 us; the launch traced here: 271 us
  Pallas kernels  258 us (94%)
  other arithmetic  7.91 us (3%)
  local copies, waits for them, and re-layouts  3.31 us (1%)
    pallas_call x1, Pallas kernels, fused_shards(): pl.pallas_call(functools.partial(fused_kernel, (requests, cores, plane, d...  258 us

profile of v4, /device:TPU:0, one launch (start us, length us, event | category | flops | bytes accessed | tf_op | source)
XLA Modules:
  0.0 271.2 jit_solution(14350457966077594576)
XLA Ops:
  1.3 0.8 multiply_bitcast_fusion
  2.1 0.8 select_reduce_fusion.1
  2.8 0.1 copy.14
  3.0 0.1 reduce
  3.1 0.1 convert_reduce_fusion
  3.2 0.6 fusion.17
  4.4 0.1 select_reduce_fusion
  4.5 0.6 bitcast_select_fusion.target_row
  5.0 1.9 fusion.9.image_from
  6.9 1.3 select_select_fusion.slot_from
  8.2 0.7 fusion.5
  9.0 0.9 pad_maximum_fusion
  9.9 258.1 %shard_map.109 = bf16[384,3072]{1,0:T(8,128)(2,1)} custom-call(bf16[512,2048]{1,0:T(8,128)(2,1)} %context.1, bf16[512,2048]{1,0:T(8,128)(2,1)} %residual.1, bf16[2048,256]{1,0:T(8,128)(2,1)} %out_weight.1, f32[1,2048]{1,0:T(1,128)} %bitcast.23, bf16[256,2048]{1,0:T(8,128)(2,1)} %bitcast.21, f32[1,4096]{1,0:T(1,128)} %bitcast.22, ...), custom_call_target="tpu_custom_call" | custom-call | flops 30000001024 | bytes 20971520 | tf_op jit(solution)/shard_map/pallas_call | solution.py:748
  268.0 3.2 %copy.18 = bf16[384,3072]{1,0:T(8,128)(2,1)} copy(bf16[384,3072]{1,0:T(8,128)(2,1)} %shard_map.109) | data formatting | bytes 4718592
  (3 shorter events, 0.1 us)

commit v5 on v4

--- a/solution.py
+++ b/solution.py
@@ -354,6 +354,26 @@
         for there, copy in near_copies(buffer, send, recv):
             pl.when(there)(copy.wait_send)
 
+    def hop_copies(buffer, send, recv, hop):
+        up, down = level + 1 < depth, level - 1 >= 0
+        if hop == 1:
+            own = buffer.at[level]
+            yield up, hand(own, send.at[0, 0], recv.at[level], level + 1)
+            yield down, hand(own, send.at[0, 1], recv.at[level], level - 1)
+        else:
+            below, above = buffer.at[level - 1], buffer.at[level + 1]
+            yield up & down, hand(below, send.at[1, 0], recv.at[level - 1], level + 1)
+            yield up & down, hand(above, send.at[1, 1], recv.at[level + 1], level - 1)
+
+    def hop_start(buffer, send, recv, hop):
+        for there, copy in hop_copies(buffer, send, recv, hop):
+            pl.when(there)(copy.start)
+
+    def hop_sent(buffer, send, recv):
+        for hop in (1, 2):
+            for there, copy in hop_copies(buffer, send, recv, hop):
+                pl.when(there)(copy.wait_send)
+
     def far_copies(buffer, send, far_recv):
         pieces = far_recv.shape[0]
         size = buffer.shape[-1] // pieces
@@ -434,24 +454,30 @@
     slab_own.wait()
     for other in others:
         arrive(slab.at[level, other], slab_in_recv.at[other])
-    near_start(slab, slab_send, slab_recv)
+    hop_start(slab, slab_send, slab_recv, 1)
 
     out_own.wait()
     for other in others:
         arrive(out_slab.at[other], out_slab_recv.at[other])
 
-    def spread(buffer, send, recv):
+    def part_of(buffer, place, part, i):
+        if i is None:
+            return buffer.at[place, part]
+        size = buffer.shape[2] // 2
+        return buffer.at[place, part, pl.ds(i * size, size)]
+
+    def spread(half_index, buffer, send, recv):
         copies = []
         for i, other in enumerate(others):
-            own = buffer.at[spot, core]
+            own = part_of(buffer, spot, core, half_index)
             copies.append(
                 remote(own, own, send.at[i], recv.at[spot, core], level * plane + other, core)
             )
             copies[-1].start()
         return copies
 
-    def cross(buffer, place, send, recv):
-        part = buffer.at[place, core]
+    def cross(half_index, buffer, place, send, recv):
+        part = part_of(buffer, place, core, half_index)
         copy = remote(part, part, send, recv.at[place, core], req, sibling)
         copy.start()
         return copy
@@ -465,8 +491,7 @@
             )
         )
         sends[-1].start()
-    sends.extend(spread(texts, text_send, text_recv))
-    sends.append(cross(texts, spot, text_cross.at[0], text_recv))
+    sends.extend(spread(0, texts, text_send.at[0], text_recv.at[0]))
 
     owner_core = level // held
     lane = level % held
@@ -524,6 +549,8 @@
 
     place_own = pltpu.make_async_copy(outgoing.at[req], arrived.at[req], place_send.at[req])
     place_own.start()
+    near_arrive(slab, slab_recv, 1)
+    hop_start(slab, slab_send, slab_recv, 2)
     place_own.wait()
 
     @pl.loop(1, requests)
@@ -542,19 +569,26 @@
     for i in range(2):
         cols = slice(i * half, (i + 1) * half)
         pictures[spot, core, :, cols] = (images[:, cols] * factor * own_gain[:, cols]).astype(BF16)
-    sends.extend(spread(pictures, picture_send, picture_recv))
-    sends.append(cross(pictures, spot, picture_cross.at[0], picture_recv))
+    sends.extend(spread(None, pictures, picture_send, picture_recv))
+    sends.extend(spread(1, texts, text_send.at[1], text_recv.at[1]))
+    sends.append(cross(None, pictures, spot, picture_cross.at[0], picture_recv))
+    for h in range(2):
+        sends.append(cross(h, texts, spot, text_cross.at[h, 0], text_recv.at[h]))
     far_start(slab, slab_recv, slab_far_send, slab_far_recv)
 
-    for i, other in enumerate(others):
-        arrive(texts.at[other, core], text_recv.at[other, core])
-        sends.append(cross(texts, other, text_cross.at[i + 1], text_recv))
+    def hand_over(h, buffer, send, recv):
+        for i, other in enumerate(others):
+            arrive(part_of(buffer, other, core, h), recv.at[other, core])
+            sends.append(cross(h, buffer, other, send.at[i + 1], recv))
+
+    for other in others:
         arrive(sources.at[other], source_recv.at[other])
-    for i, other in enumerate(others):
-        arrive(pictures.at[other, core], picture_recv.at[other, core])
-        sends.append(cross(pictures, other, picture_cross.at[i + 1], picture_recv))
+    hand_over(0, texts, text_cross.at[0], text_recv.at[0])
+    hand_over(None, pictures, picture_cross, picture_recv)
+    hand_over(1, texts, text_cross.at[1], text_recv.at[1])
     for place in [spot] + others:
-        arrive(texts.at[place, sibling], text_recv.at[place, sibling])
+        for h in range(2):
+            arrive(part_of(texts, place, sibling, h), text_recv.at[h, place, sibling])
         arrive(pictures.at[place, sibling], picture_recv.at[place, sibling])
 
     tile = 256
@@ -591,7 +625,8 @@
 
     multiply_all(level, True)
     for d in (1, 2):
-        near_arrive(slab, slab_recv, d)
+        if d == 2:
+            near_arrive(slab, slab_recv, d)
 
         @pl.when(level - d >= 0)
         def _():
@@ -653,7 +688,7 @@
         copy.wait_send()
     near_sent(blocks, block_send, block_recv)
     far_sent(blocks, block_far_send, block_far_recv)
-    near_sent(slab, slab_send, slab_recv)
+    hop_sent(slab, slab_send, slab_recv)
     far_sent(slab, slab_far_send, slab_far_recv)
 
     @pl.loop(0, depth)
@@ -785,9 +820,9 @@
             dma((requests,)),
             dma((2,)),
             dma((2,)),
-            dma((plane,)),
-            dma((plane, cores)),
-            dma((plane,)),
+            dma((2, plane)),
+            dma((2, plane, cores)),
+            dma((2, plane)),
             dma((plane,)),
             dma((plane, cores)),
             dma((plane,)),

time: 274 us -> 236 us (0.86)
  Pallas kernels: 258 us -> 219 us
    pallas_call x1, Pallas kernels: 258 us -> 219 us  [fused_shards(): pl.pallas_call(functools.partial(fused_kernel, (requests, cores, plane, d...]
where the time goes in v5:
time: 236 us; the launch traced here: 232 us
  Pallas kernels  219 us (93%)
  other arithmetic  7.91 us (3%)
  local copies, waits for them, and re-layouts  3.31 us (1%)
    pallas_call x1, Pallas kernels, fused_shards(): pl.pallas_call(functools.partial(fused_kernel, (requests, cores, plane, d...  219 us

profile of v5, /device:TPU:0, one launch (start us, length us, event | category | flops | bytes accessed | tf_op | source)
XLA Modules:
  0.0 231.9 jit_solution(12837371911489441723)
XLA Ops:
  1.3 0.8 multiply_bitcast_fusion
  2.1 0.8 select_reduce_fusion.1
  2.8 0.1 copy.14
  3.0 0.1 reduce
  3.1 0.1 convert_reduce_fusion
  3.2 0.6 fusion.17
  4.4 0.1 select_reduce_fusion
  4.5 0.6 bitcast_select_fusion.target_row
  5.0 1.9 fusion.9.image_from
  6.9 1.3 select_select_fusion.slot_from
  8.2 0.7 fusion.5
  9.0 0.9 pad_maximum_fusion
  9.9 218.8 %shard_map.109 = bf16[384,3072]{1,0:T(8,128)(2,1)} custom-call(bf16[512,2048]{1,0:T(8,128)(2,1)} %context.1, bf16[512,2048]{1,0:T(8,128)(2,1)} %residual.1, bf16[2048,256]{1,0:T(8,128)(2,1)} %out_weight.1, f32[1,2048]{1,0:T(1,128)} %bitcast.23, bf16[256,2048]{1,0:T(8,128)(2,1)} %bitcast.21, f32[1,4096]{1,0:T(1,128)} %bitcast.22, ...), custom_call_target="tpu_custom_call" | custom-call | flops 30000001024 | bytes 20971520 | tf_op jit(solution)/shard_map/pallas_call | solution.py:783
  228.6 3.2 %copy.18 = bf16[384,3072]{1,0:T(8,128)(2,1)} copy(bf16[384,3072]{1,0:T(8,128)(2,1)} %shard_map.109) | data formatting | bytes 4718592
  (3 shorter events, 0.1 us)

commit v6 on v5

--- a/solution.py
+++ b/solution.py
@@ -549,6 +549,7 @@
 
     place_own = pltpu.make_async_copy(outgoing.at[req], arrived.at[req], place_send.at[req])
     place_own.start()
+    sends.extend(spread(1, texts, text_send.at[1], text_recv.at[1]))
     near_arrive(slab, slab_recv, 1)
     hop_start(slab, slab_send, slab_recv, 2)
     place_own.wait()
@@ -570,7 +571,6 @@
         cols = slice(i * half, (i + 1) * half)
         pictures[spot, core, :, cols] = (images[:, cols] * factor * own_gain[:, cols]).astype(BF16)
     sends.extend(spread(None, pictures, picture_send, picture_recv))
-    sends.extend(spread(1, texts, text_send.at[1], text_recv.at[1]))
     sends.append(cross(None, pictures, spot, picture_cross.at[0], picture_recv))
     for h in range(2):
         sends.append(cross(h, texts, spot, text_cross.at[h, 0], text_recv.at[h]))
@@ -584,8 +584,8 @@
     for other in others:
         arrive(sources.at[other], source_recv.at[other])
     hand_over(0, texts, text_cross.at[0], text_recv.at[0])
+    hand_over(1, texts, text_cross.at[1], text_recv.at[1])
     hand_over(None, pictures, picture_cross, picture_recv)
-    hand_over(1, texts, text_cross.at[1], text_recv.at[1])
     for place in [spot] + others:
         for h in range(2):
             arrive(part_of(texts, place, sibling, h), text_recv.at[h, place, sibling])

time: 236 us -> 224 us (0.949)
  the two profiles are of different devices: /device:TPU:0 before, /device:TPU:17 now
where the time goes in v6:
time: 224 us
  Pallas kernels  211 us (94%)
  other arithmetic  7.91 us (4%)
  local copies, waits for them, and re-layouts  3.31 us (1%)
    pallas_call x1, Pallas kernels, fused_shards(): pl.pallas_call(functools.partial(fused_kernel, (requests, cores, plane, d...  211 us

profile of v6, /device:TPU:17, one launch (start us, length us, event | category | flops | bytes accessed | tf_op | source)
XLA Modules:
  0.0 224.2 jit_solution(1885823636159815559)
XLA Ops:
  1.3 0.8 multiply_bitcast_fusion
  2.1 0.8 select_reduce_fusion.1
  2.8 0.1 copy.14
  3.0 0.1 reduce
  3.1 0.1 convert_reduce_fusion
  3.2 0.6 fusion.17
  4.4 0.1 select_reduce_fusion
  4.5 0.6 bitcast_select_fusion.target_row
  5.0 1.9 fusion.9.image_from
  6.9 1.3 select_select_fusion.slot_from
  8.2 0.7 fusion.5
  9.0 0.9 pad_maximum_fusion
  9.9 211.1 %shard_map.109 = bf16[384,3072]{1,0:T(8,128)(2,1)} custom-call(bf16[512,2048]{1,0:T(8,128)(2,1)} %context.1, bf16[512,2048]{1,0:T(8,128)(2,1)} %residual.1, bf16[2048,256]{1,0:T(8,128)(2,1)} %out_weight.1, f32[1,2048]{1,0:T(1,128)} %bitcast.23, bf16[256,2048]{1,0:T(8,128)(2,1)} %bitcast.21, f32[1,4096]{1,0:T(1,128)} %bitcast.22, ...), custom_call_target="tpu_custom_call" | custom-call | flops 30000001024 | bytes 20971520 | tf_op jit(solution)/shard_map/pallas_call | solution.py:783
  220.9 3.2 %copy.18 = bf16[384,3072]{1,0:T(8,128)(2,1)} copy(bf16[384,3072]{1,0:T(8,128)(2,1)} %shard_map.109) | data formatting | bytes 4718592
  (3 shorter events, 0.1 us)
